TPU v7x, 256 devices: a whole 4x4x8 slice. The times are simulated.
256 devices in a mesh: dp: 64 (over y_lo, x, z), tensor: 4 (over y_hi, core).
Axes of the slice: x: 4, y: 4 (y_hi: 2, y_lo: 2; y = y_hi * 2 + y_lo), z: 8, core: 2. Of those that a mesh axis runs over, the one named last changes fastest.
Arguments:
- tokens: bfloat16 [512, 3072], P(('dp', 'tensor')), may hold values from -6 to 6
- target: bfloat16 [512, 3072], P(('dp', 'tensor')), may hold values from -6 to 6
- master_up: float32 [24576, 3072], P(('dp', 'tensor')), may hold values from -0.109375 to 0.109375
- master_down: float32 [24576, 3072], P(('dp', 'tensor')), may hold values from -0.0390625 to 0.0390625
- tangent_up: bfloat16 [24576, 3072], P(('dp', 'tensor')), may hold values from -5 to 5
- tangent_down: bfloat16 [24576, 3072], P(('dp', 'tensor')), may hold values from -5 to 5
- moment_up: bfloat16 [24576, 3072], P(('dp', 'tensor')), may hold values from -0.15625 to 0.15625
- moment_down: bfloat16 [24576, 3072], P(('dp', 'tensor')), may hold values from -0.15625 to 0.15625
- curve_up: bfloat16 [24576, 3072], P(('dp', 'tensor')), may hold values from 0.19921875 to 4
- curve_down: bfloat16 [24576, 3072], P(('dp', 'tensor')), may hold values from 0.19921875 to 4
Outputs:
- step_up: float32 [24576, 3072], P(('dp', 'tensor'))
- step_down: float32 [24576, 3072], P(('dp', 'tensor'))
- moment_up_next: bfloat16 [24576, 3072], P(('dp', 'tensor'))
- moment_down_next: bfloat16 [24576, 3072], P(('dp', 'tensor'))
- curve_up_next: bfloat16 [24576, 3072], P(('dp', 'tensor'))
- curve_down_next: bfloat16 [24576, 3072], P(('dp', 'tensor'))
All inputs are finite; a program needn't handle non-finite values.
Results may differ from a plain program's by a relative error of at most 0.009.
Values may be sent and summed in bfloat16 or wider, within the bound.
A program may use at most 128 MiB of HBM per device.

v0:
```python
import math

import jax
import jax.numpy as jnp
from jax import lax
from jax.sharding import PartitionSpec as P

TOKENS = 512


beta_first = 0.965
beta_second = 0.99
gamma_scale = 0.01
ratio_floor = 0.01
root_half = 0.7071067811865476
inv_root_tau = 0.3989422804014327


def gelu_parts(pre_act):
    normal_cdf = 0.5 * (1.0 + lax.erf(pre_act * root_half))
    density = jnp.exp(-0.5 * pre_act * pre_act) * inv_root_tau
    return (
        pre_act * normal_cdf,
        normal_cdf + pre_act * density,
        density * (2.0 - pre_act * pre_act),
    )


def times_transposed(left, right):
    return lax.dot_general(
        left, right, (((1,), (1,)), ((), ())), preferred_element_type=jnp.float32
    )


def transposed_times(left, right):
    return lax.dot_general(
        left, right, (((0,), (0,)), ((), ())), preferred_element_type=jnp.float32
    )


def refresh(moment, curve, grad, hvp, tangent):
    moment_f = beta_first * moment.astype(jnp.float32) + (1.0 - beta_first) * grad
    curve_f = (
        beta_second * curve.astype(jnp.float32)
        + (1.0 - beta_second) * tangent.astype(jnp.float32) * hvp
    )
    step = jnp.clip(moment_f / jnp.maximum(gamma_scale * curve_f, ratio_floor), -1.0, 1.0)
    return (step, moment_f.astype(jnp.bfloat16), curve_f.astype(jnp.bfloat16))


def per_device(
    tokens,
    target,
    master_up,
    master_down,
    tangent_up,
    tangent_down,
    moment_up,
    moment_down,
    curve_up,
    curve_down,
):
    loss_scale = 1.0 / math.sqrt(TOKENS)
    weight_up = master_up.astype(jnp.bfloat16)
    weight_down = master_down.astype(jnp.bfloat16)
    features = weight_down.shape[1]
    all_tokens = lax.all_gather(tokens, ("dp", "tensor"), axis=0, tiled=True)
    pre_act = times_transposed(all_tokens, weight_up)
    pre_tangent = times_transposed(all_tokens, tangent_up)
    activated, slopes, bending = gelu_parts(pre_act)
    hidden = activated.astype(jnp.bfloat16)
    hidden_dot = (slopes * pre_tangent).astype(jnp.bfloat16)
    hidden_rows = hidden
    hidden_dot_rows = hidden_dot
    primal = jnp.dot(hidden_rows, weight_down, preferred_element_type=jnp.float32)
    moved = jnp.dot(hidden_dot_rows, weight_down, preferred_element_type=jnp.float32) + jnp.dot(
        hidden_rows, tangent_down, preferred_element_type=jnp.float32
    )
    summed = lax.psum_scatter(
        jnp.concatenate([primal, moved], axis=1), ("dp", "tensor"), scatter_dimension=0, tiled=True
    )
    residual_pair = jnp.concatenate(
        [
            (summed[:, :features] - target.astype(jnp.float32)).astype(jnp.bfloat16),
            summed[:, features:].astype(jnp.bfloat16),
        ],
        axis=1,
    )
    block_rows = lax.all_gather(residual_pair, ("dp", "tensor"), axis=0, tiled=True)
    piece_res = block_rows[:, :features]
    piece_dot = block_rows[:, features:]
    hidden_rows = hidden
    hidden_dot_rows = hidden_dot
    back_grad = times_transposed(piece_res, weight_down)
    back_dot = times_transposed(piece_dot, weight_down) + times_transposed(piece_res, tangent_down)
    grad_pre = (back_grad * slopes).astype(jnp.bfloat16)
    grad_pre_dot = (back_dot * slopes + back_grad * bending * pre_tangent).astype(jnp.bfloat16)
    step_up, moment_up_next, curve_up_next = refresh(
        moment_up,
        curve_up,
        loss_scale * transposed_times(grad_pre, all_tokens),
        loss_scale * transposed_times(grad_pre_dot, all_tokens),
        tangent_up,
    )
    step_down, moment_down_next, curve_down_next = refresh(
        moment_down,
        curve_down,
        loss_scale * transposed_times(hidden_rows, piece_res),
        loss_scale
        * (transposed_times(hidden_dot_rows, piece_res) + transposed_times(hidden_rows, piece_dot)),
        tangent_down,
    )
    return (step_up, step_down, moment_up_next, moment_down_next, curve_up_next, curve_down_next)


def solution(mesh):
    in_specs = (
        P(("dp", "tensor"), None),
        P(("dp", "tensor"), None),
        P(("dp", "tensor"), None),
        P(("dp", "tensor"), None),
        P(("dp", "tensor"), None),
        P(("dp", "tensor"), None),
        P(("dp", "tensor"), None),
        P(("dp", "tensor"), None),
        P(("dp", "tensor"), None),
        P(("dp", "tensor"), None),
    )
    out_specs = (
        P(("dp", "tensor"), None),
        P(("dp", "tensor"), None),
        P(("dp", "tensor"), None),
        P(("dp", "tensor"), None),
        P(("dp", "tensor"), None),
        P(("dp", "tensor"), None),
    )
    return jax.shard_map(
        per_device, mesh=mesh, in_specs=in_specs, out_specs=out_specs, check_vma=False
    )
```

profile of v0, /device:TPU:1, one launch (start us, length us, event | category | flops | bytes accessed | tf_op | source)
XLA Modules:
  0.0 1199.4 jit_solution(15928170086471492067)
XLA Ops:
  7.2 0.7 all-gather.5.cloned.1.call-update
  7.9 2.2 convert_element_type.58
  10.1 415.5 %all-gather.5.cloned.1.call-done = bf16[256,2,3072]{2,1,0:T(2,128)(2,1)} async-done(((bf16[1,2,3072]{2,1,0:T(2,128)(2,1)}), bf16[256,2,3072]{2,1,0:T(2,128)(2,1)}) %all-gather.5.cloned.1.call-update) | async-done | bytes 3145744 | tf_op jit(solution)/shard_map/all_gather | solution.py:67
  425.6 6.3 reshape.13
  432.0 2.4 fusion.31
  434.4 1.1 fusion.58
  435.5 3.6 fusion.53
  439.2 1.0 fusion.52
  440.2 3.6 convolution_add_fusion
  443.8 10.6 pad_maximum_fusion
  454.7 284.3 %all-reduce.3.cloned.1.call-done = f32[512,6144]{1,0:T(8,128)} async-done(((f32[512,6144]{1,0:T(8,128)}), f32[512,6144]{1,0:T(8,128)}) %all-reduce.3.cloned.1.call-update) | async-done | bytes 12582928
  739.1 1.0 dynamic-slice.7
  740.0 0.9 fusion.46
  741.0 0.6 maximum_bitcast_fusion
  741.6 417.9 %all-gather.7.cloned.1.call-done = bf16[256,2,6144]{2,1,0:T(2,128)(2,1)} async-done(((bf16[1,2,6144]{2,1,0:T(2,128)(2,1)}), bf16[256,2,6144]{2,1,0:T(2,128)(2,1)}) %all-gather.7.cloned.1.call-update) | async-done | bytes 6291472 | tf_op jit(solution)/shard_map/all_gather | solution.py:89
  1159.5 13.3 %reshape.15 = bf16[512,6144]{1,0:T(8,128)(2,1)} reshape(bf16[256,2,6144]{2,1,0:T(2,128)(2,1)} %all-gather.7.cloned.1.call-done) | data formatting | bytes 12582912
  1172.8 2.6 fusion.10
  1175.5 3.1 fusion.15
  1178.6 0.6 copy-done
  1179.2 1.8 fusion.8
  1181.0 0.7 fusion.3
  1182.1 1.7 fusion.6
  1183.8 2.5 fusion.54
  1186.3 6.6 fusion.55
  (26 shorter events, 0.7 us)
Async XLA Ops:
  7.2 418.4 %all-gather.5.cloned.1.call-start = ((), (), s32[]{:S(2)}) async-start(), calls=%async_computation | async-start | bytes 3158016 | tf_op jit(solution)/shard_map/all_gather | solution.py:67
  7.9 731.2 %all-reduce.3.cloned.1.call-start = ((), (), s32[]{:S(2)}) async-start(), calls=%async_computation.2 | async-start | bytes 25165824
  431.9 2.5 copy-start.6
  434.4 1.1 copy-start.1
  439.2 1.1 copy-start.3
  454.5 285.6 %copy-start.8 = (bf16[2,3072]{1,0:T(2,128)(2,1)S(1)}, bf16[2,3072]{1,0:T(2,128)(2,1)}, u32[]{:S(2)}) copy-start(bf16[2,3072]{1,0:T(2,128)(2,1)} %param.11) | copy-start | bytes 36868
  454.5 705.0 %all-gather.7.cloned.1.call-start = ((), (), s32[]{:S(2)}) async-start(), calls=%async_computation.1 | async-start | bytes 6316032 | tf_op jit(solution)/shard_map/all_gather | solution.py:89
  1172.8 2.6 copy-start.2
  1175.4 3.7 copy-start
  1179.2 2.5 copy-start.7
  1179.2 1.8 copy-start.9
  1181.0 1.1 copy-start.5
  1182.1 1.7 copy-start.4
  1182.1 1.7 copy-start.10
Sparse Core Ops, SparseCore 0:
  9.9 415.6 all-gather.4
  454.6 284.3 all-reduce.2
  741.7 417.7 all-gather.6
where the time goes:
time: 1200 us
  waiting for transfers between devices  1120 us (93%)
  matrix products  30.9 us (3%)
  local copies, waits for them, and re-layouts  21.6 us (2%)
  other arithmetic  14.3 us (1%)
  between operations  13.9 us (1%)
    all_gather x1, waiting for transfers between devices, per_device(): lax.all_gather(residual_pair, ('dp', 'tensor'), axis=0, tiled=True)  418 us
    all_gather x1, waiting for transfers between devices, per_device(): all_tokens = lax.all_gather(tokens, ('dp', 'tensor'), axis=0, tiled=True)  416 us
    unnamed x4, waiting for transfers between devices  285 us
  transfers between devices with their start and end apart: 3, of which 3 were waited for; matrix products, arithmetic and copies ran while one was open for 0% of the time, Pallas kernels for 0%

commit v1 on v0

v1 whole, which is shorter than its diff:
```python
import math

import jax
import jax.numpy as jnp
from jax import lax
from jax.experimental import pallas as pl
from jax.experimental.pallas import tpu as pltpu
from jax.sharding import PartitionSpec as P

TOKENS = 512
D = 3072
HID = 96
PAD = 128
PARTS = 3
SIZE = {"y": 4, "x": 4, "z": 8}
AXES = ("y", "x", "z")
GATHER_ORDER = (("y", "z", "x"), ("z", "x", "y"), ("x", "y", "z"))
PART_ORDER = (2, 0, 1)
GROUP = 8
WIDE = D // GROUP
BLOCK = WIDE // PARTS

beta_first = 0.965
beta_second = 0.99
gamma_scale = 0.01
ratio_floor = 0.01
root_half = 0.7071067811865476
inv_root_tau = 0.3989422804014327

F32 = jnp.float32
BF16 = jnp.bfloat16
MESH = pl.DeviceIdType.MESH


def gelu_parts(pre_act):
    normal_cdf = 0.5 * (1.0 + lax.erf(pre_act * root_half))
    density = jnp.exp(-0.5 * pre_act * pre_act) * inv_root_tau
    return (
        pre_act * normal_cdf,
        normal_cdf + pre_act * density,
        density * (2.0 - pre_act * pre_act),
    )


def refresh(moment, curve, grad, hvp, tangent):
    moment_f = beta_first * moment.astype(F32) + (1.0 - beta_first) * grad
    curve_f = beta_second * curve.astype(F32) + (1.0 - beta_second) * tangent.astype(F32) * hvp
    step = jnp.clip(moment_f / jnp.maximum(gamma_scale * curve_f, ratio_floor), -1.0, 1.0)
    return step, moment_f.astype(BF16), curve_f.astype(BF16)


def wrap(value, size):
    return lax.rem(value + size, size)


def device(pos):
    y = pos["y"]
    return (
        lax.rem(y, 2) * 32 + pos["x"] * 8 + pos["z"],
        lax.div(y, 2) * 2 + pos["c"],
    )


def beside(pos, axis, by):
    return device({**pos, axis: wrap(pos[axis] + by, SIZE[axis])})


def place(where):
    return tuple(where[axis] for axis in AXES)


def halved(where, fulls, which):
    axis = fulls[0]
    half = SIZE[axis] // 2
    return {**where, axis: pl.ds(which * half, half)}


def gather_messages():
    table, count = {}, 0
    for part in range(PARTS):
        for phase, axis in enumerate(GATHER_ORDER[part]):
            for hop in range(SIZE[axis] // 2):
                for side in (1, -1):
                    table[(part, phase, hop, side)] = count
                    count += 1
        for number in range(SIZE[GATHER_ORDER[part][2]]):
            table[(part, number)] = count
            count += 1
    return table, count


GATHER_TABLE, GATHER_COUNT = gather_messages()


def scatter_messages():
    table, count = {}, 0
    for part in range(PARTS):
        for phase, axis in enumerate(GATHER_ORDER[part][::-1]):
            for hop in range(SIZE[axis] // 2):
                for side in (1, -1):
                    table[(part, phase, hop, side)] = count
                    count += 1
    return table, count


SCATTER_TABLE, SCATTER_COUNT = scatter_messages()


def gather_part(part, buffer, pos, send_sems, recv_sems, sent):
    mine = buffer.at[part, pos["c"]]
    other = buffer.at[part, 1 - pos["c"]]
    sibling = device({**pos, "c": 1 - pos["c"]})

    def copy(index, ref, target):
        return pltpu.make_async_remote_copy(
            src_ref=ref,
            dst_ref=ref,
            send_sem=send_sems.at[index],
            recv_sem=recv_sems.at[index],
            device_id=target,
            device_id_type=MESH,
        )

    def start(index, ref, target):
        made = copy(index, ref, target)
        made.start()
        sent.append(made)

    fulls = []
    arrivals = []
    for phase, axis in enumerate(GATHER_ORDER[part]):
        size = SIZE[axis]
        half = size // 2
        at = pos[axis]

        def chunk(offset, side=None):
            where = {**pos, axis: wrap(at + offset, size)}
            for full in fulls:
                where[full] = slice(None)
            if side is not None:
                where = halved(where, fulls, 0 if side == 1 else 1)
            return place(where)

        def moving(hop, side, behind):
            last = hop == half - 1
            if last and not fulls and side == -1:
                return None
            split = side if last and fulls else None
            return chunk(-side * (hop + behind), split)

        def await_hop(hop):
            for side in (1, -1):
                where = moving(hop, side, 1)
                if where is not None:
                    index = GATHER_TABLE[(part, phase, hop, side)]
                    copy(index, mine.at[where], sibling).wait_recv()

        def hand_on(offset, number):
            where = chunk(offset)
            index = GATHER_TABLE[(part, number)]
            start(index, mine.at[where], sibling)
            arrivals.append((index, where))

        for hop in range(half):
            if hop > 0:
                await_hop(hop - 1)
            for side in (1, -1):
                where = moving(hop, side, 0)
                if where is not None:
                    index = GATHER_TABLE[(part, phase, hop, side)]
                    start(index, mine.at[where], beside(pos, axis, side))
            if phase == 2:
                hand_on(-hop, 2 * hop)
                if hop > 0:
                    hand_on(hop, 2 * hop - 1)
            yield
        await_hop(half - 1)
        if phase == 2:
            hand_on(half, size - 1)
        fulls = [name for name in AXES if name in fulls or name == axis]
    yield
    for index, where in arrivals:
        copy(index, other.at[where], sibling).wait_recv()


def scatter_part(part, sums, boxes, pos, send_sems, recv_sems, sent):
    mine = sums.at[part]
    order = GATHER_ORDER[part][::-1]
    fulls = [name for name in AXES]
    for phase, axis in enumerate(order):
        size = SIZE[axis]
        half = size // 2
        at = pos[axis]
        box = boxes[part * 3 + phase]
        fulls = [name for name in fulls if name != axis]

        def chunk(offset, side=None):
            where = {**pos, axis: wrap(at + offset, size)}
            for full in fulls:
                where[full] = slice(None)
            if side is not None:
                where = halved(where, fulls, 0 if side == 1 else 1)
            return place(where)

        def slot(hop, side, split):
            where = {name: slice(None) for name in fulls}
            if split:
                where = halved(where, fulls, 0 if side == 1 else 1)
            lead = (0 if side == 1 else 1, hop)
            return lead + tuple(where[name] for name in AXES if name in fulls)

        def describe(hop, side):
            last = hop == half - 1
            if last and not fulls and side == -1:
                return None
            split = last and bool(fulls)
            return split, slot(hop, side, split)

        def copy(hop, side, source, into):
            index = SCATTER_TABLE[(part, phase, hop, side)]
            return pltpu.make_async_remote_copy(
                src_ref=mine.at[source],
                dst_ref=box.at[into],
                send_sem=send_sems.at[index],
                recv_sem=recv_sems.at[index],
                device_id=beside(pos, axis, side),
                device_id_type=MESH,
            )

        for hop in range(half - 1, -1, -1):
            for side in (1, -1):
                if hop < half - 1:
                    came = describe(hop + 1, side)
                    if came is not None:
                        split, into = came
                        where = chunk(side * (hop + 1), side if split else None)
                        copy(hop + 1, side, where, into).wait_recv()
                        mine[where] = (mine[where].astype(F32) + box[into].astype(F32)).astype(BF16)
                goes = describe(hop, side)
                if goes is not None:
                    split, into = goes
                    where = chunk(side * (hop + 1), side if split else None)
                    made = copy(hop, side, where, into)
                    made.start()
                    sent.append(made)
            yield
        where = chunk(0)
        total = mine[where].astype(F32)
        for side in (1, -1):
            split, into = describe(0, side)
            copy(0, side, where, into).wait_recv()
            total = total + box[into].astype(F32)
        if phase < 2:
            mine[where] = total.astype(BF16)
        else:
            yield total
            return


def together(runs):
    alive = dict(runs)
    result = {}
    while alive:
        for part in list(alive):
            try:
                result[part] = next(alive[part])
            except StopIteration:
                del alive[part]
    return result


def kernel(
    tokens,
    target,
    master_up,
    master_down,
    tangent_up,
    tangent_down,
    moment_up,
    moment_down,
    curve_up,
    curve_down,
    step_up,
    step_down,
    moment_up_next,
    moment_down_next,
    curve_up_next,
    curve_down_next,
    v_master_up,
    v_master_down,
    v_tangent_up,
    v_tangent_down,
    v_moment_up,
    v_moment_down,
    v_curve_up,
    v_curve_down,
    o_step_up,
    o_step_down,
    o_moment_up,
    o_moment_down,
    o_curve_up,
    o_curve_down,
    group,
    goal,
    all_tokens,
    weights_up,
    weights_down,
    acc,
    both,
    both_t,
    grads_t,
    slopes_ref,
    bend_ref,
    outgoing,
    incoming,
    sums,
    residuals,
    *rest,
):
    boxes = rest[: 3 * PARTS]
    in_sems, out_sems, pair_send, pair_recv, group_send, group_recv = rest[9:15]
    first_send, first_recv, scatter_send, scatter_recv, second_send, second_recv = rest[15:]

    dp = lax.axis_index("dp")
    tensor = lax.axis_index("tensor")
    core = lax.rem(tensor, 2)
    pos = {
        "x": lax.rem(lax.div(dp, 8), 4),
        "z": lax.rem(dp, 8),
        "y": lax.div(tensor, 2) * 2 + lax.div(dp, 32),
        "c": core,
    }
    me = core * 4 + pos["y"]
    sent = []

    loads = []
    pairs = (
        (master_up, v_master_up),
        (tangent_up, v_tangent_up),
        (master_down, v_master_down),
        (tangent_down, v_tangent_down),
        (moment_up, v_moment_up),
        (moment_down, v_moment_down),
        (curve_up, v_curve_up),
        (curve_down, v_curve_down),
    )
    for number, (source, into) in enumerate(pairs):
        made = pltpu.make_async_copy(source, into, in_sems.at[number])
        made.start()
        loads.append(made)

    def member(by):
        spot = lax.rem(me + by, GROUP)
        return device({**pos, "c": lax.div(spot, 4), "y": lax.rem(spot, 4)})

    barrier = pltpu.get_barrier_semaphore()
    peers = [member(by) for by in range(1, GROUP)]
    peers += [beside(pos, axis, side) for axis in ("x", "z") for side in (1, -1)]
    for peer in peers:
        pl.semaphore_signal(barrier, inc=1, device_id=peer, device_id_type=MESH)

    rows = jnp.concatenate([tokens[...].astype(F32), target[...].astype(F32)], axis=0)
    pieces = []
    for lead in (0, 2):
        pieces.append(
            jnp.concatenate(
                [rows[lead : lead + 2, k * WIDE : (k + 1) * WIDE] for k in range(GROUP)], axis=0
            )
        )
    group[me] = jnp.concatenate(pieces, axis=1).astype(BF16)
    pl.semaphore_wait(barrier, len(peers))

    def group_copy(by, spot):
        return pltpu.make_async_remote_copy(
            src_ref=group.at[spot],
            dst_ref=group.at[spot],
            send_sem=group_send.at[by],
            recv_sem=group_recv.at[by],
            device_id=member(by),
            device_id_type=MESH,
        )

    for by in range(1, GROUP):
        made = group_copy(by, me)
        made.start()
        sent.append(made)

    for made in loads[:4]:
        made.wait()
    zeros_up = jnp.zeros((PAD - HID, 768), BF16)
    for k in range(4):
        columns = slice(k * 768, (k + 1) * 768)
        weights_up[k, 0:HID] = v_master_up[:, columns].astype(BF16)
        weights_up[k, HID:PAD] = zeros_up
        weights_up[k, PAD : PAD + HID] = v_tangent_up[:, columns]
        weights_up[k, PAD + HID :] = zeros_up
    zeros_low = jnp.zeros((PAD - HID, 2 * BLOCK), BF16)
    zeros_half = jnp.zeros((HID, BLOCK), BF16)
    for spot in range(GROUP):
        for part in range(PARTS):
            start = spot * WIDE + part * BLOCK
            columns = slice(start, start + BLOCK)
            into = weights_down.at[part, spot // 4, spot % 4]
            weight = v_master_down[:, columns].astype(BF16)
            into[0:HID, 0:BLOCK] = weight
            into[0:HID, BLOCK:] = v_tangent_down[:, columns]
            into[HID:PAD] = zeros_low
            into[PAD : PAD + HID, 0:BLOCK] = zeros_half
            into[PAD : PAD + HID, BLOCK:] = weight
            into[PAD + HID :] = zeros_low

    for by in range(1, GROUP):
        group_copy(by, lax.rem(me + GROUP - by, GROUP)).wait_recv()
    row = lax.broadcasted_iota(jnp.int32, (16, 128), 0)
    column = lax.broadcasted_iota(jnp.int32, (16, 128), 1)
    pick = (column == lax.div(row, 2) * 16 + me * 2 + lax.rem(row, 2)).astype(F32).astype(BF16)
    picked = jnp.dot(pick, group[...].reshape(128, 2 * WIDE), preferred_element_type=F32)
    goal[...] = picked[:, WIDE:]
    for part in range(PARTS):
        own = all_tokens.at[part, core, pos["y"], pos["x"], pos["z"]]
        own[...] = picked[:, part * BLOCK : (part + 1) * BLOCK].astype(BF16)

    together(
        (part, gather_part(part, all_tokens, pos, first_send, first_recv, sent))
        for part in PART_ORDER
    )

    acc[...] = jnp.zeros_like(acc)

    @pl.loop(0, 4)
    def _(k):
        spot = 2 * k
        blocks = []
        for lower in range(2):
            for part in range(PARTS):
                block = all_tokens[part, lax.div(spot, 4), lax.rem(spot, 4) + lower]
                blocks.append(block.reshape(TOKENS, BLOCK))
        acc[...] += lax.dot_general(
            jnp.concatenate(blocks, axis=1),
            weights_up[k],
            (((1,), (1,)), ((), ())),
            preferred_element_type=F32,
        )

    @pl.loop(0, 4)
    def _(k):
        span = pl.ds(pl.multiple_of(k * 128, 128), 128)
        pre_tangent = acc[span, PAD:]
        activated, slopes, bending = gelu_parts(acc[span, :PAD])
        slopes_ref[span] = slopes
        bend_ref[span] = bending * pre_tangent
        pair = jnp.concatenate([activated, slopes * pre_tangent], axis=1)
        both[span] = pair.astype(BF16)

    sibling = device({**pos, "c": 1 - core})

    def pair_copy(part):
        return pltpu.make_async_remote_copy(
            src_ref=outgoing.at[part],
            dst_ref=incoming.at[part],
            send_sem=pair_send.at[part],
            recv_sem=pair_recv.at[part],
            device_id=sibling,
            device_id_type=MESH,
        )

    for part in PART_ORDER:

        @pl.loop(0, 4)
        def _(y):
            block = jnp.dot(
                both[...], weights_down[part, 1 - core, y], preferred_element_type=F32
            )
            outgoing[part, y] = block.astype(BF16).reshape(4, 8, 16, 2 * BLOCK)

        made = pair_copy(part)
        made.start()
        sent.append(made)

    scatters = {}
    for part in PART_ORDER:
        pair_copy(part).wait_recv()

        @pl.loop(0, 4)
        def _(y):
            block = jnp.dot(both[...], weights_down[part, core, y], preferred_element_type=F32)
            block = block + incoming[part, y].astype(F32).reshape(TOKENS, 2 * BLOCK)
            sums[part, y] = block.astype(BF16).reshape(4, 8, 16, 2 * BLOCK)

        scatters[part] = scatter_part(part, sums, boxes, pos, scatter_send, scatter_recv, sent)
        next(scatters[part])

    both_t[...] = both[...].astype(F32).T.astype(BF16)
    totals = together(scatters.items())
    for part in PART_ORDER:
        total = totals[part]
        residual = total[:, :BLOCK] - goal[:, part * BLOCK : (part + 1) * BLOCK]
        own = residuals.at[part, core, pos["y"], pos["x"], pos["z"]]
        own[...] = jnp.concatenate([total[:, BLOCK:], residual], axis=1).astype(BF16)

    together(
        (part, gather_part(part, residuals, pos, second_send, second_recv, sent))
        for part in PART_ORDER
    )

    acc[...] = jnp.zeros_like(acc)

    @pl.loop(0, GROUP)
    def _(spot):
        half, y = lax.div(spot, 4), lax.rem(spot, 4)
        left = [residuals[part, half, y].reshape(TOKENS, 2 * BLOCK) for part in range(PARTS)]
        right = [weights_down[part, half, y] for part in range(PARTS)]
        acc[...] += lax.dot_general(
            jnp.concatenate(left, axis=1),
            jnp.concatenate(right, axis=1),
            (((1,), (1,)), ((), ())),
            preferred_element_type=F32,
        )

    for k in range(4):
        span = slice(k * 128, (k + 1) * 128)
        back_dot, back_grad = acc[span, :PAD], acc[span, PAD:]
        slopes = slopes_ref[span]
        grad_pre = (back_grad * slopes).T.astype(BF16)
        grad_pre_dot = (back_dot * slopes + back_grad * bend_ref[span]).T.astype(BF16)
        grads_t[0:PAD, span] = grad_pre
        grads_t[PAD:, span] = grad_pre_dot

    for made in loads[4:]:
        made.wait()
    loss_scale = 1.0 / math.sqrt(TOKENS)
    results = (
        (o_step_up, step_up),
        (o_step_down, step_down),
        (o_moment_up, moment_up_next),
        (o_moment_down, moment_down_next),
        (o_curve_up, curve_up_next),
        (o_curve_down, curve_down_next),
    )

    def store(number, spot):
        source, into = results[number]
        span = pl.ds(pl.multiple_of(spot * WIDE, 128), WIDE)
        return pltpu.make_async_copy(
            source.at[:, span], into.at[:, span], out_sems.at[number, spot]
        )

    @pl.loop(0, GROUP)
    def _(spot):
        half, y = lax.div(spot, 4), lax.rem(spot, 4)
        span = pl.ds(pl.multiple_of(spot * WIDE, 128), WIDE)
        right = [all_tokens[part, half, y].reshape(TOKENS, BLOCK) for part in range(PARTS)]
        up = jnp.dot(
            grads_t[...], jnp.concatenate(right, axis=1), preferred_element_type=F32
        )
        o_step_up[:, span], o_moment_up[:, span], o_curve_up[:, span] = refresh(
            v_moment_up[:, span],
            v_curve_up[:, span],
            loss_scale * up[:HID],
            loss_scale * up[PAD : PAD + HID],
            v_tangent_up[:, span],
        )
        grad, hvp = [], []
        for part in range(PARTS):
            down = jnp.dot(
                both_t[...],
                residuals[part, half, y].reshape(TOKENS, 2 * BLOCK),
                preferred_element_type=F32,
            )
            grad.append(down[:HID, BLOCK:])
            hvp.append(down[:HID, :BLOCK] + down[PAD : PAD + HID, BLOCK:])
        o_step_down[:, span], o_moment_down[:, span], o_curve_down[:, span] = refresh(
            v_moment_down[:, span],
            v_curve_down[:, span],
            loss_scale * jnp.concatenate(grad, axis=1),
            loss_scale * jnp.concatenate(hvp, axis=1),
            v_tangent_down[:, span],
        )
        for number in range(6):
            store(number, spot).start()

    for made in sent:
        made.wait_send()

    @pl.loop(0, GROUP)
    def _(spot):
        for number in range(6):
            store(number, spot).wait()


def box_shapes():
    shapes = []
    for part in range(PARTS):
        fulls = list(AXES)
        for axis in GATHER_ORDER[part][::-1]:
            fulls.remove(axis)
            lead = (2, SIZE[axis] // 2) + tuple(SIZE[name] for name in fulls)
            shapes.append(pltpu.VMEM(lead + (16, 2 * BLOCK), BF16))
    return shapes


def per_device(*arrays):
    wide32 = jax.ShapeDtypeStruct((HID, D), F32)
    wide16 = jax.ShapeDtypeStruct((HID, D), BF16)
    blocks = (4, 4, 8, 16)
    any_spec = pl.BlockSpec(memory_space=pl.ANY)
    scratch = [pltpu.VMEM((HID, D), F32)] * 2 + [pltpu.VMEM((HID, D), BF16)] * 6
    scratch += [pltpu.VMEM((HID, D), F32)] * 2 + [pltpu.VMEM((HID, D), BF16)] * 4
    scratch += [
        pltpu.VMEM((GROUP, 16, 2 * WIDE), BF16),
        pltpu.VMEM((16, WIDE), F32),
        pltpu.VMEM((PARTS, 2) + blocks + (BLOCK,), BF16),
        pltpu.VMEM((4, 2 * PAD, 768), BF16),
        pltpu.VMEM((PARTS, 2, 4, 2 * PAD, 2 * BLOCK), BF16),
        pltpu.VMEM((TOKENS, 2 * PAD), F32),
        pltpu.VMEM((TOKENS, 2 * PAD), BF16),
        pltpu.VMEM((2 * PAD, TOKENS), BF16),
        pltpu.VMEM((2 * PAD, TOKENS), BF16),
        pltpu.VMEM((TOKENS, PAD), F32),
        pltpu.VMEM((TOKENS, PAD), F32),
        pltpu.VMEM((PARTS,) + blocks + (2 * BLOCK,), BF16),
        pltpu.VMEM((PARTS,) + blocks + (2 * BLOCK,), BF16),
        pltpu.VMEM((PARTS,) + blocks + (2 * BLOCK,), BF16),
        pltpu.VMEM((PARTS, 2) + blocks + (2 * BLOCK,), BF16),
    ]
    scratch += box_shapes()
    dma = pltpu.SemaphoreType.DMA
    scratch += [
        dma((8,)),
        dma((6, GROUP)),
        dma((PARTS,)),
        dma((PARTS,)),
        dma((GROUP,)),
        dma((GROUP,)),
        dma((GATHER_COUNT,)),
        dma((GATHER_COUNT,)),
        dma((SCATTER_COUNT,)),
        dma((SCATTER_COUNT,)),
        dma((GATHER_COUNT,)),
        dma((GATHER_COUNT,)),
    ]
    return pl.pallas_call(
        kernel,
        out_shape=(wide32, wide32, wide16, wide16, wide16, wide16),
        in_specs=[pl.BlockSpec(memory_space=pltpu.VMEM)] * 2 + [any_spec] * 8,
        out_specs=(any_spec,) * 6,
        scratch_shapes=scratch,
        compiler_params=pltpu.CompilerParams(
            collective_id=0, has_side_effects=True, vmem_limit_bytes=60 * 1024 * 1024
        ),
        cost_estimate=pl.CostEstimate(
            flops=4_000_000_000, bytes_accessed=11_000_000, transcendentals=131072
        ),
    )(*arrays)


def solution(mesh):
    rows = P(("dp", "tensor"), None)
    return jax.shard_map(
        per_device, mesh=mesh, in_specs=(rows,) * 10, out_specs=(rows,) * 6, check_vma=False
    )
```

time: 1200 us -> 140 us (0.12)
  waiting for transfers between devices: 1120 us -> 0 us
  Pallas kernels: 0 us -> 132 us
  matrix products: 30.9 us -> 0 us
  other arithmetic: 14.3 us -> 0 us
  local copies, waits for them, and re-layouts: 21.6 us -> 7.65 us
  between operations: 13.9 us -> 0.66 us
    all_gather x2 -> x0, waiting for transfers between devices: 833 us -> none  [the longest x1 418 us: per_device(): lax.all_gather(residual_pair, ('dp', 'tensor'), axis=0, tiled=True)]
    unnamed x4 -> x0, waiting for transfers between devices: 285 us -> none
    pallas_call x0 -> x1, Pallas kernels: none -> 132 us  [per_device(): pl.pallas_call(kernel, out_shape=(wide32, wide32, wide16, wide16, wide16,...]
    dot_general x12 -> x0, matrix products: 30.9 us -> none  [the longest x5 14.1 us: transposed_times(): lax.dot_general(left, right, (((0,), (0,)), ((), ())), preferred_element_...]
    unnamed x24 -> x16, local copies, waits for them, and re-layouts: 20.6 us -> 7.65 us
  transfers between devices with their start and end apart: 3 -> 0, of which waited for: 3 -> 0; matrix products, arithmetic and copies ran while one was open for 0% -> 0% of each run, Pallas kernels for 0% -> 0%
where the time goes in v1:
time: 140 us
  Pallas kernels  132 us (94%)
  local copies, waits for them, and re-layouts  7.65 us (5%)
    pallas_call x1, Pallas kernels, per_device(): pl.pallas_call(kernel, out_shape=(wide32, wide32, wide16, wide16, wide16,...  132 us
    unnamed x16, local copies, waits for them, and re-layouts  7.65 us

profile of v1, /device:TPU:1, one launch (start us, length us, event | category | flops | bytes accessed | tf_op | source)
XLA Modules:
  0.0 139.9 jit_solution(11305414868159463537)
XLA Ops:
  0.6 131.6 %shard_map.145 = (f32[96,3072]{1,0:T(8,128)}, f32[96,3072]{1,0:T(8,128)}, bf16[96,3072]{1,0:T(8,128)(2,1)}, bf16[96,3072]{1,0:T(8,128)(2,1)}, bf16[96,3072]{1,0:T(8,128)(2,1)}, /*index=5*/bf16[96,3072]{1,0:T(8,128)(2,1)}) custom-call(bf16[2,3072]{1,0:T(2,128)(2,1)} %tokens.1, bf16[2,3072]{1,0:T(2,128)(2,1)} %target.1, f32[96,3072]{1,0:T(8,128)} %master_up.1, ...), custom_call_target="tpu_custom_call" | custom-call | flops 4000000000 | bytes 11000000 | tf_op jit(solution)/shard_map/pallas_call | solution.py:642
  132.2 0.0 copy-start
  132.2 2.5 %copy.22 = f32[96,3072]{1,0:T(8,128)} copy(f32[96,3072]{1,0:T(8,128)} %get-tuple-element.12) | data formatting | bytes 2359296
  134.7 0.0 copy-done
  134.7 0.0 copy-start.4
  134.7 1.0 copy.23
  135.7 0.5 copy-done.4
  136.2 0.0 copy-start.3
  136.2 0.0 copy-start.2
  136.2 0.8 copy.24
  137.0 0.5 copy-done.3
  137.4 0.0 copy-start.1
  137.4 0.8 copy.25
  138.3 0.0 copy-done.2
  138.3 0.8 copy.26
  139.1 0.0 copy-done.1
  139.1 0.8 copy.27
Async XLA Ops:
  132.2 2.5 %copy-start = (f32[96,3072]{1,0:T(8,128)S(1)}, f32[96,3072]{1,0:T(8,128)}, u32[]{:S(2)}) copy-start(f32[96,3072]{1,0:T(8,128)} %get-tuple-element.13) | copy-start | bytes 3538948
  134.7 1.5 %copy-start.4 = (bf16[96,3072]{1,0:T(8,128)(2,1)S(1)}, bf16[96,3072]{1,0:T(8,128)(2,1)}, u32[]{:S(2)}) copy-start(bf16[96,3072]{1,0:T(8,128)(2,1)} %get-tuple-element.14) | copy-start | bytes 1769476
  136.2 1.3 copy-start.3
  136.2 2.1 %copy-start.2 = (bf16[96,3072]{1,0:T(8,128)(2,1)S(1)}, bf16[96,3072]{1,0:T(8,128)(2,1)}, u32[]{:S(2)}) copy-start(bf16[96,3072]{1,0:T(8,128)(2,1)} %get-tuple-element.16) | copy-start | bytes 1769476
  137.4 1.6 %copy-start.1 = (bf16[96,3072]{1,0:T(8,128)(2,1)S(1)}, bf16[96,3072]{1,0:T(8,128)(2,1)}, u32[]{:S(2)}) copy-start(bf16[96,3072]{1,0:T(8,128)(2,1)} %get-tuple-element.17) | copy-start | bytes 1769476

commit v2 on v1

v2 whole, which is shorter than its diff:
```python
import math

import jax
import jax.numpy as jnp
from jax import lax
from jax.experimental import pallas as pl
from jax.experimental.pallas import tpu as pltpu
from jax.sharding import PartitionSpec as P

TOKENS = 512
D = 3072
HID = 96
PAD = 128
PARTS = 3
SIZE = {"y": 4, "x": 4, "z": 8}
AXES = ("y", "x", "z")
GROUP = 8
WIDE = D // GROUP
NEAR = (2, 1, 3)
LONG = (4, 3, 5, 2, 6, 1, 7)
PARTS = (("y", "x"), ("x", "y"))
GATHER_COUNT = 7 + 2 * 15 + 2 * 16
SCATTER_COUNT = 2 * (12 + 3) + 7

beta_first = 0.965
beta_second = 0.99
gamma_scale = 0.01
ratio_floor = 0.01
root_half = 0.7071067811865476
inv_root_tau = 0.3989422804014327

F32 = jnp.float32
BF16 = jnp.bfloat16
MESH = pl.DeviceIdType.MESH


def gelu_parts(pre_act):
    normal_cdf = 0.5 * (1.0 + lax.erf(pre_act * root_half))
    density = jnp.exp(-0.5 * pre_act * pre_act) * inv_root_tau
    return (
        pre_act * normal_cdf,
        normal_cdf + pre_act * density,
        density * (2.0 - pre_act * pre_act),
    )


def refresh(moment, curve, grad, hvp, tangent):
    moment_f = beta_first * moment.astype(F32) + (1.0 - beta_first) * grad
    curve_f = beta_second * curve.astype(F32) + (1.0 - beta_second) * tangent.astype(F32) * hvp
    step = jnp.clip(moment_f / jnp.maximum(gamma_scale * curve_f, ratio_floor), -1.0, 1.0)
    return step, moment_f.astype(BF16), curve_f.astype(BF16)


def wrap(value, size):
    return lax.rem(value + size, size)


def device(pos):
    y = pos["y"]
    return (
        lax.rem(y, 2) * 32 + pos["x"] * 8 + pos["z"],
        lax.div(y, 2) * 2 + pos["c"],
    )


def beside(pos, axis, by):
    return device({**pos, axis: wrap(pos[axis] + by, SIZE[axis])})


def place(where):
    return tuple(where[axis] for axis in AXES)


def half_rows(part):
    return pl.ds(part * 4, 4)


def gather(buffer, pos, send_sems, recv_sems, sent):
    mine = buffer.at[pos["c"]]
    other = buffer.at[1 - pos["c"]]
    sibling = device({**pos, "c": 1 - pos["c"]})

    def copy(index, ref, target):
        return pltpu.make_async_remote_copy(
            src_ref=ref,
            dst_ref=ref,
            send_sem=send_sems.at[index],
            recv_sem=recv_sems.at[index],
            device_id=target,
            device_id_type=MESH,
        )

    def start(index, ref, target):
        made = copy(index, ref, target)
        made.start()
        sent.append(made)

    def block(part, back_middle, back_final):
        middle, final = PARTS[part]
        where = {
            middle: wrap(pos[middle] - back_middle, 4),
            final: wrap(pos[final] - back_final, 4),
            "z": half_rows(part),
        }
        return place(where)

    def hand_on(part, m, f):
        start(37 + part * 16 + m * 4 + f, mine.at[block(part, m, f)], sibling)

    own = mine.at[place(pos)]
    for by in LONG:
        start(by - 1, own, beside(pos, "z", by))
    yield
    for by in LONG[::-1]:
        came = mine.at[place({**pos, "z": wrap(pos["z"] - by, 8)})]
        copy(by - 1, came, sibling).wait_recv()
    for part in range(2):
        for m in NEAR:
            start(7 + part * 15 + m - 1, mine.at[block(part, 0, 0)], beside(pos, PARTS[part][0], m))
    for part in range(2):
        for f in NEAR:
            start(10 + part * 15 + f - 1, mine.at[block(part, 0, 0)], beside(pos, PARTS[part][1], f))
        hand_on(part, 0, 0)
    for m in (1, 3, 2):
        for part in range(2):
            came = mine.at[block(part, m, 0)]
            copy(7 + part * 15 + m - 1, came, sibling).wait_recv()
            for f in NEAR:
                index = 13 + part * 15 + (m - 1) * 3 + f - 1
                start(index, came, beside(pos, PARTS[part][1], f))
            hand_on(part, m, 0)
    for m in (0, 1, 3, 2):
        for f in (1, 3, 2):
            for part in range(2):
                index = (10 if m == 0 else 13 + (m - 1) * 3) + part * 15 + f - 1
                copy(index, mine.at[block(part, m, f)], sibling).wait_recv()
                hand_on(part, m, f)
    for m in (0, 1, 3, 2):
        for f in (0, 1, 3, 2):
            for part in range(2):
                index = 37 + part * 16 + m * 4 + f
                copy(index, other.at[block(part, m, f)], sibling).wait_recv()


class Scatter:
    def __init__(self, sums, boxes, pos, send_sems, recv_sems, sent):
        self.sums, self.boxes, self.pos = sums, boxes, pos
        self.send_sems, self.recv_sems, self.sent = send_sems, recv_sems, sent

    def copy(self, index, source, into, target):
        return pltpu.make_async_remote_copy(
            src_ref=source,
            dst_ref=into,
            send_sem=self.send_sems.at[index],
            recv_sem=self.recv_sems.at[index],
            device_id=target,
            device_id_type=MESH,
        )

    def start(self, *what):
        made = self.copy(*what)
        made.start()
        self.sent.append(made)

    def piece(self, part, by_first, by_second):
        second, first = PARTS[part]
        where = {
            first: wrap(self.pos[first] + by_first, 4),
            second: wrap(self.pos[second] + by_second, 4),
            "z": half_rows(part),
        }
        return place(where)

    def first(self, part, by_first, by_second):
        index = part * 15 + (by_first - 1) * 4 + by_second
        self.start(
            index,
            self.sums.at[self.piece(part, by_first, by_second)],
            self.boxes[0].at[part, by_first - 1, by_second],
            beside(self.pos, PARTS[part][1], by_first),
        )

    def second(self, part, by_second):
        box = self.boxes[0]
        where = self.piece(part, 0, by_second)
        total = self.sums[where].astype(F32)
        for by in (1, 3, 2):
            index = part * 15 + (by - 1) * 4 + by_second
            into = box.at[part, by - 1, by_second]
            self.copy(index, self.sums.at[where], into, beside(self.pos, "x", 1)).wait_recv()
            total = total + box[part, by - 1, by_second].astype(F32)
        if by_second:
            self.sums[where] = total.astype(BF16)
            self.start(
                part * 15 + 12 + by_second - 1,
                self.sums.at[where],
                self.boxes[1].at[part, by_second - 1],
                beside(self.pos, PARTS[part][0], by_second),
            )
            return
        for by in (1, 3, 2):
            into = self.boxes[1].at[part, by - 1]
            index = part * 15 + 12 + by - 1
            self.copy(index, self.sums.at[where], into, beside(self.pos, "x", 1)).wait_recv()
            total = total + self.boxes[1][part, by - 1].astype(F32)
        self.sums[where] = total.astype(BF16)

    def third(self):
        for by in LONG:
            self.start(
                30 + by - 1,
                self.sums.at[place({**self.pos, "z": wrap(self.pos["z"] + by, 8)})],
                self.boxes[2].at[by - 1],
                beside(self.pos, "z", by),
            )
        where = place(self.pos)
        total = self.sums[where].astype(F32)
        for by in LONG[::-1]:
            into = self.boxes[2].at[by - 1]
            self.copy(30 + by - 1, self.sums.at[where], into, beside(self.pos, "x", 1)).wait_recv()
            total = total + self.boxes[2][by - 1].astype(F32)
        return total


def kernel(
    tokens,
    target,
    master_up,
    master_down,
    tangent_up,
    tangent_down,
    moment_up,
    moment_down,
    curve_up,
    curve_down,
    step_up,
    step_down,
    moment_up_next,
    moment_down_next,
    curve_up_next,
    curve_down_next,
    v_master_up,
    v_master_down,
    v_tangent_up,
    v_tangent_down,
    v_moment_up,
    v_moment_down,
    v_curve_up,
    v_curve_down,
    o_step_up,
    o_step_down,
    o_moment_up,
    o_moment_down,
    o_curve_up,
    o_curve_down,
    group,
    folded,
    all_tokens,
    weights_up,
    weights_down,
    acc,
    both,
    both_t,
    grads_t,
    slopes_ref,
    bend_ref,
    outgoing,
    incoming,
    sums,
    residuals,
    *rest,
):
    boxes = rest[:3]
    in_sems, out_sems, pair_send, pair_recv, group_send, group_recv = rest[3:9]
    first_send, first_recv, scatter_send, scatter_recv, second_send, second_recv = rest[9:]

    dp = lax.axis_index("dp")
    tensor = lax.axis_index("tensor")
    core = lax.rem(tensor, 2)
    pos = {
        "x": lax.rem(lax.div(dp, 8), 4),
        "z": lax.rem(dp, 8),
        "y": lax.div(tensor, 2) * 2 + lax.div(dp, 32),
        "c": core,
    }
    me = core * 4 + pos["y"]
    sent = []

    loads = []
    pairs = (
        (master_up, v_master_up),
        (tangent_up, v_tangent_up),
        (master_down, v_master_down),
        (tangent_down, v_tangent_down),
        (moment_up, v_moment_up),
        (moment_down, v_moment_down),
        (curve_up, v_curve_up),
        (curve_down, v_curve_down),
    )
    for number, (source, into) in enumerate(pairs):
        made = pltpu.make_async_copy(source, into, in_sems.at[number])
        made.start()
        loads.append(made)

    def member(by):
        spot = lax.rem(me + by, GROUP)
        return device({**pos, "c": lax.div(spot, 4), "y": lax.rem(spot, 4)})

    barrier = pltpu.get_barrier_semaphore()
    peers = [member(by) for by in range(1, GROUP)]
    peers += [beside(pos, "x", by) for by in range(1, 4)]
    peers += [beside(pos, "z", by) for by in range(1, 8)]
    for peer in peers:
        pl.semaphore_signal(barrier, inc=1, device_id=peer, device_id_type=MESH)

    def fold(rows):
        rows = rows.astype(F32)
        pieces = [rows[:, k * WIDE : (k + 1) * WIDE] for k in range(GROUP)]
        return jnp.concatenate(pieces, axis=0).astype(BF16)

    folded[core, pos["y"], pos["x"], pos["z"]] = fold(tokens[...])
    group[me] = fold(target[...])

    loads[0].wait()
    loads[1].wait()
    zeros_up = jnp.zeros((PAD - HID, 768), BF16)
    for k in range(4):
        columns = slice(k * 768, (k + 1) * 768)
        weights_up[k, 0:HID] = v_master_up[:, columns].astype(BF16)
        weights_up[k, HID:PAD] = zeros_up
        weights_up[k, PAD : PAD + HID] = v_tangent_up[:, columns]
        weights_up[k, PAD + HID :] = zeros_up
    pl.semaphore_wait(barrier, len(peers))

    first = gather(folded, pos, first_send, first_recv, sent)
    next(first)

    def group_copy(by, spot):
        return pltpu.make_async_remote_copy(
            src_ref=group.at[spot],
            dst_ref=group.at[spot],
            send_sem=group_send.at[by],
            recv_sem=group_recv.at[by],
            device_id=member(by),
            device_id_type=MESH,
        )

    for by in range(1, GROUP):
        made = group_copy(by, me)
        made.start()
        sent.append(made)

    loads[2].wait()
    loads[3].wait()
    zeros_low = jnp.zeros((PAD - HID, 2 * WIDE), BF16)
    zeros_half = jnp.zeros((HID, WIDE), BF16)
    for spot in range(GROUP):
        columns = slice(spot * WIDE, (spot + 1) * WIDE)
        weight = v_master_down[:, columns].astype(BF16)
        weights_down[spot, 0:HID, 0:WIDE] = weight
        weights_down[spot, 0:HID, WIDE:] = v_tangent_down[:, columns]
        weights_down[spot, HID:PAD] = zeros_low
        weights_down[spot, PAD : PAD + HID, 0:WIDE] = zeros_half
        weights_down[spot, PAD : PAD + HID, WIDE:] = weight
        weights_down[spot, PAD + HID :] = zeros_low

    for _ in first:
        pass

    row = lax.broadcasted_iota(jnp.int32, (128, 128), 0)
    column = lax.broadcasted_iota(jnp.int32, (128, 128), 1)
    token = lax.rem(row, 16)
    pick = column == lax.div(token, 2) * 16 + lax.div(row, 16) * 2 + lax.rem(token, 2)
    pick = pick.astype(F32).astype(BF16)

    @pl.loop(0, 4)
    def _(x):
        for z in range(8):
            blocks = folded[:, :, x, z].reshape(128, WIDE)
            rows = jnp.dot(pick, blocks, preferred_element_type=F32).astype(BF16)
            all_tokens[:, x, z] = rows.reshape(GROUP, 16, WIDE)

    acc[...] = jnp.zeros_like(acc)

    @pl.loop(0, 4)
    def _(k):
        blocks = [all_tokens[2 * k + lower].reshape(TOKENS, WIDE) for lower in range(2)]
        acc[...] += lax.dot_general(
            jnp.concatenate(blocks, axis=1),
            weights_up[k],
            (((1,), (1,)), ((), ())),
            preferred_element_type=F32,
        )

    @pl.loop(0, 4)
    def _(k):
        span = pl.ds(pl.multiple_of(k * 128, 128), 128)
        pre_tangent = acc[span, PAD:]
        activated, slopes, bending = gelu_parts(acc[span, :PAD])
        slopes_ref[span] = slopes
        bend_ref[span] = bending * pre_tangent
        pair = jnp.concatenate([activated, slopes * pre_tangent], axis=1)
        both[span] = pair.astype(BF16)

    sibling = device({**pos, "c": 1 - core})

    def pair_copy(by):
        return pltpu.make_async_remote_copy(
            src_ref=outgoing.at[by],
            dst_ref=incoming.at[by],
            send_sem=pair_send.at[by],
            recv_sem=pair_recv.at[by],
            device_id=sibling,
            device_id_type=MESH,
        )

    turns = (1, 3, 2, 0)
    for by in turns:
        spot = (1 - core) * 4 + wrap(pos["y"] + by, 4)
        block = jnp.dot(both[...], weights_down[spot], preferred_element_type=F32)
        outgoing[by] = block.astype(BF16).reshape(4, 8, 16, 2 * WIDE)
        made = pair_copy(by)
        made.start()
        sent.append(made)

    scatter = Scatter(sums, boxes, pos, scatter_send, scatter_recv, sent)
    for by in turns:
        pair_copy(by).wait_recv()
        y = wrap(pos["y"] + by, 4)
        block = jnp.dot(both[...], weights_down[core * 4 + y], preferred_element_type=F32)
        block = block + incoming[by].astype(F32).reshape(TOKENS, 2 * WIDE)
        sums[y] = block.astype(BF16).reshape(4, 8, 16, 2 * WIDE)
        for to in NEAR:
            scatter.first(0, to, by)
        if by:
            for to in turns:
                scatter.first(1, by, to)

    both_t[...] = both[...].astype(F32).T.astype(BF16)
    for by in turns:
        for part in range(2):
            scatter.second(part, by)
    total = scatter.third()

    for by in range(1, GROUP):
        group_copy(by, lax.rem(me + GROUP - by, GROUP)).wait_recv()
    row = lax.broadcasted_iota(jnp.int32, (16, 128), 0)
    column = lax.broadcasted_iota(jnp.int32, (16, 128), 1)
    pick = (column == lax.div(row, 2) * 16 + me * 2 + lax.rem(row, 2)).astype(F32).astype(BF16)
    goal = jnp.dot(pick, group[...].reshape(128, WIDE), preferred_element_type=F32)
    pair = jnp.concatenate([total[:, WIDE:], total[:, :WIDE] - goal], axis=1)
    residuals[core, pos["y"], pos["x"], pos["z"]] = pair.astype(BF16)

    for _ in gather(residuals, pos, second_send, second_recv, sent):
        pass

    acc[...] = jnp.zeros_like(acc)

    @pl.loop(0, GROUP)
    def _(spot):
        acc[...] += lax.dot_general(
            residuals[lax.div(spot, 4), lax.rem(spot, 4)].reshape(TOKENS, 2 * WIDE),
            weights_down[spot],
            (((1,), (1,)), ((), ())),
            preferred_element_type=F32,
        )

    for k in range(4):
        span = slice(k * 128, (k + 1) * 128)
        back_dot, back_grad = acc[span, :PAD], acc[span, PAD:]
        slopes = slopes_ref[span]
        grad_pre = (back_grad * slopes).T.astype(BF16)
        grad_pre_dot = (back_dot * slopes + back_grad * bend_ref[span]).T.astype(BF16)
        grads_t[0:PAD, span] = grad_pre
        grads_t[PAD:, span] = grad_pre_dot

    for made in loads[4:]:
        made.wait()
    loss_scale = 1.0 / math.sqrt(TOKENS)
    results = (
        (o_step_up, step_up),
        (o_step_down, step_down),
        (o_moment_up, moment_up_next),
        (o_moment_down, moment_down_next),
        (o_curve_up, curve_up_next),
        (o_curve_down, curve_down_next),
    )

    def store(number, spot):
        source, into = results[number]
        span = pl.ds(pl.multiple_of(spot * WIDE, 128), WIDE)
        return pltpu.make_async_copy(
            source.at[:, span], into.at[:, span], out_sems.at[number, spot]
        )

    @pl.loop(0, GROUP)
    def _(spot):
        span = pl.ds(pl.multiple_of(spot * WIDE, 128), WIDE)
        up = jnp.dot(
            grads_t[...], all_tokens[spot].reshape(TOKENS, WIDE), preferred_element_type=F32
        )
        o_step_up[:, span], o_moment_up[:, span], o_curve_up[:, span] = refresh(
            v_moment_up[:, span],
            v_curve_up[:, span],
            loss_scale * up[:HID],
            loss_scale * up[PAD : PAD + HID],
            v_tangent_up[:, span],
        )
        down = jnp.dot(
            both_t[...],
            residuals[lax.div(spot, 4), lax.rem(spot, 4)].reshape(TOKENS, 2 * WIDE),
            preferred_element_type=F32,
        )
        o_step_down[:, span], o_moment_down[:, span], o_curve_down[:, span] = refresh(
            v_moment_down[:, span],
            v_curve_down[:, span],
            loss_scale * down[:HID, WIDE:],
            loss_scale * (down[:HID, :WIDE] + down[PAD : PAD + HID, WIDE:]),
            v_tangent_down[:, span],
        )
        for number in range(6):
            store(number, spot).start()

    for made in sent:
        made.wait_send()

    @pl.loop(0, GROUP)
    def _(spot):
        for number in range(6):
            store(number, spot).wait()


def per_device(*arrays):
    wide32 = jax.ShapeDtypeStruct((HID, D), F32)
    wide16 = jax.ShapeDtypeStruct((HID, D), BF16)
    blocks = (4, 4, 8, 16)
    any_spec = pl.BlockSpec(memory_space=pl.ANY)
    scratch = [pltpu.VMEM((HID, D), F32)] * 2 + [pltpu.VMEM((HID, D), BF16)] * 6
    scratch += [pltpu.VMEM((HID, D), F32)] * 2 + [pltpu.VMEM((HID, D), BF16)] * 4
    scratch += [
        pltpu.VMEM((GROUP, 16, WIDE), BF16),
        pltpu.VMEM((2,) + blocks + (WIDE,), BF16),
        pltpu.VMEM((GROUP, 4, 8, 16, WIDE), BF16),
        pltpu.VMEM((4, 2 * PAD, 768), BF16),
        pltpu.VMEM((GROUP, 2 * PAD, 2 * WIDE), BF16),
        pltpu.VMEM((TOKENS, 2 * PAD), F32),
        pltpu.VMEM((TOKENS, 2 * PAD), BF16),
        pltpu.VMEM((2 * PAD, TOKENS), BF16),
        pltpu.VMEM((2 * PAD, TOKENS), BF16),
        pltpu.VMEM((TOKENS, PAD), F32),
        pltpu.VMEM((TOKENS, PAD), F32),
        pltpu.VMEM(blocks + (2 * WIDE,), BF16),
        pltpu.VMEM(blocks + (2 * WIDE,), BF16),
        pltpu.VMEM(blocks + (2 * WIDE,), BF16),
        pltpu.VMEM((2,) + blocks + (2 * WIDE,), BF16),
        pltpu.VMEM((2, 3, 4, 4, 16, 2 * WIDE), BF16),
        pltpu.VMEM((2, 3, 4, 16, 2 * WIDE), BF16),
        pltpu.VMEM((7, 16, 2 * WIDE), BF16),
    ]
    dma = pltpu.SemaphoreType.DMA
    scratch += [
        dma((8,)),
        dma((6, GROUP)),
        dma((4,)),
        dma((4,)),
        dma((GROUP,)),
        dma((GROUP,)),
        dma((GATHER_COUNT,)),
        dma((GATHER_COUNT,)),
        dma((SCATTER_COUNT,)),
        dma((SCATTER_COUNT,)),
        dma((GATHER_COUNT,)),
        dma((GATHER_COUNT,)),
    ]
    return pl.pallas_call(
        kernel,
        out_shape=(wide32, wide32, wide16, wide16, wide16, wide16),
        in_specs=[pl.BlockSpec(memory_space=pltpu.VMEM)] * 2 + [any_spec] * 8,
        out_specs=(any_spec,) * 6,
        scratch_shapes=scratch,
        compiler_params=pltpu.CompilerParams(
            collective_id=0, has_side_effects=True, vmem_limit_bytes=60 * 1024 * 1024
        ),
        cost_estimate=pl.CostEstimate(
            flops=4_000_000_000, bytes_accessed=11_000_000, transcendentals=131072
        ),
    )(*arrays)


def solution(mesh):
    rows = P(("dp", "tensor"), None)
    return jax.shard_map(
        per_device, mesh=mesh, in_specs=(rows,) * 10, out_specs=(rows,) * 6, check_vma=False
    )
```

time: 140 us -> 116 us (0.83)
  Pallas kernels: 132 us -> 107 us
    pallas_call x1, Pallas kernels: 132 us -> 107 us  [per_device(): pl.pallas_call(kernel, out_shape=(wide32, wide32, wide16, wide16, wide16,...]
where the time goes in v2:
time: 116 us
  Pallas kernels  107 us (92%)
  local copies, waits for them, and re-layouts  7.65 us (7%)
    pallas_call x1, Pallas kernels, per_device(): pl.pallas_call(kernel, out_shape=(wide32, wide32, wide16, wide16, wide16,...  107 us
    unnamed x16, local copies, waits for them, and re-layouts  7.65 us

profile of v2, /device:TPU:1, one launch (start us, length us, event | category | flops | bytes accessed | tf_op | source)
XLA Modules:
  0.0 115.8 jit_solution(1688775708082040551)
XLA Ops:
  0.6 107.5 %shard_map.145 = (f32[96,3072]{1,0:T(8,128)}, f32[96,3072]{1,0:T(8,128)}, bf16[96,3072]{1,0:T(8,128)(2,1)}, bf16[96,3072]{1,0:T(8,128)(2,1)}, bf16[96,3072]{1,0:T(8,128)(2,1)}, /*index=5*/bf16[96,3072]{1,0:T(8,128)(2,1)}) custom-call(bf16[2,3072]{1,0:T(2,128)(2,1)} %tokens.1, bf16[2,3072]{1,0:T(2,128)(2,1)} %target.1, f32[96,3072]{1,0:T(8,128)} %master_up.1, ...), custom_call_target="tpu_custom_call" | custom-call | flops 4000000000 | bytes 11000000 | tf_op jit(solution)/shard_map/pallas_call | solution.py:575
  108.1 0.0 copy-start
  108.1 2.5 %copy.22 = f32[96,3072]{1,0:T(8,128)} copy(f32[96,3072]{1,0:T(8,128)} %get-tuple-element.12) | data formatting | bytes 2359296
  110.6 0.0 copy-done
  110.6 0.0 copy-start.4
  110.6 1.0 copy.23
  111.6 0.5 copy-done.4
  112.1 0.0 copy-start.3
  112.1 0.0 copy-start.2
  112.1 0.8 copy.24
  112.9 0.5 copy-done.3
  113.3 0.0 copy-start.1
  113.3 0.8 copy.25
  114.2 0.0 copy-done.2
  114.2 0.8 copy.26
  115.0 0.0 copy-done.1
  115.0 0.8 copy.27
Async XLA Ops:
  108.1 2.5 %copy-start = (f32[96,3072]{1,0:T(8,128)S(1)}, f32[96,3072]{1,0:T(8,128)}, u32[]{:S(2)}) copy-start(f32[96,3072]{1,0:T(8,128)} %get-tuple-element.13) | copy-start | bytes 3538948
  110.6 1.5 %copy-start.4 = (bf16[96,3072]{1,0:T(8,128)(2,1)S(1)}, bf16[96,3072]{1,0:T(8,128)(2,1)}, u32[]{:S(2)}) copy-start(bf16[96,3072]{1,0:T(8,128)(2,1)} %get-tuple-element.14) | copy-start | bytes 1769476
  112.1 1.3 %copy-start.3 = (bf16[96,3072]{1,0:T(8,128)(2,1)S(1)}, bf16[96,3072]{1,0:T(8,128)(2,1)}, u32[]{:S(2)}) copy-start(bf16[96,3072]{1,0:T(8,128)(2,1)} %get-tuple-element.15) | copy-start | bytes 1769476
  112.1 2.1 %copy-start.2 = (bf16[96,3072]{1,0:T(8,128)(2,1)S(1)}, bf16[96,3072]{1,0:T(8,128)(2,1)}, u32[]{:S(2)}) copy-start(bf16[96,3072]{1,0:T(8,128)(2,1)} %get-tuple-element.16) | copy-start | bytes 1769476
  113.3 1.6 %copy-start.1 = (bf16[96,3072]{1,0:T(8,128)(2,1)S(1)}, bf16[96,3072]{1,0:T(8,128)(2,1)}, u32[]{:S(2)}) copy-start(bf16[96,3072]{1,0:T(8,128)(2,1)} %get-tuple-element.17) | copy-start | bytes 1769476

commit v3 on v2

v3 whole, which is shorter than its diff:
```python
import math

import jax
import jax.numpy as jnp
from jax import lax
from jax.experimental import pallas as pl
from jax.experimental.pallas import tpu as pltpu
from jax.sharding import PartitionSpec as P

TOKENS = 512
D = 3072
HID = 96
PAD = 128
PARTS = 3
SIZE = {"y": 4, "x": 4, "z": 8}
AXES = ("y", "x", "z")
GROUP = 8
WIDE = D // GROUP
NEAR = (2, 1, 3)
PARTS = (("y", "x"), ("x", "y"))
OFFSETS = (0, 1, 7, 6, 2, 3, 5, 4)
PAIRS = ((0, 0, 2), (1, 2, 2), (0, 4, 2), (1, 6, 2))
SETS = ((0, 0, 1), (0, 1, 1), (1, 2, 1), (1, 3, 1), (0, 4, 2), (1, 6, 2))
GATHER_COUNT = 7 + 6 * 15 + 4
SCATTER_COUNT = 4 * 15 + 7

beta_first = 0.965
beta_second = 0.99
gamma_scale = 0.01
ratio_floor = 0.01
root_half = 0.7071067811865476
inv_root_tau = 0.3989422804014327

F32 = jnp.float32
BF16 = jnp.bfloat16
MESH = pl.DeviceIdType.MESH


def gelu_parts(pre_act):
    normal_cdf = 0.5 * (1.0 + lax.erf(pre_act * root_half))
    density = jnp.exp(-0.5 * pre_act * pre_act) * inv_root_tau
    return (
        pre_act * normal_cdf,
        normal_cdf + pre_act * density,
        density * (2.0 - pre_act * pre_act),
    )


def refresh(moment, curve, grad, hvp, tangent):
    moment_f = beta_first * moment.astype(F32) + (1.0 - beta_first) * grad
    curve_f = beta_second * curve.astype(F32) + (1.0 - beta_second) * tangent.astype(F32) * hvp
    step = jnp.clip(moment_f / jnp.maximum(gamma_scale * curve_f, ratio_floor), -1.0, 1.0)
    return step, moment_f.astype(BF16), curve_f.astype(BF16)


def wrap(value, size):
    return lax.rem(value + size, size)


class Here:
    def __init__(self):
        dp = lax.axis_index("dp")
        tensor = lax.axis_index("tensor")
        self.core = lax.rem(tensor, 2)
        self.pos = {
            "x": lax.rem(lax.div(dp, 8), 4),
            "z": lax.rem(dp, 8),
            "y": lax.div(tensor, 2) * 2 + lax.div(dp, 32),
        }
        self.me = self.core * 4 + self.pos["y"]
        self.steps = {
            (axis, by): wrap(self.pos[axis] + by, SIZE[axis])
            for axis in AXES
            for by in range(SIZE[axis])
        }
        self.devices = {
            key: self.device({**self.pos, key[0]: spot}, self.core)
            for key, spot in self.steps.items()
            if key[1]
        }
        self.sibling = self.device(self.pos, 1 - self.core)

    def device(self, pos, core):
        y = pos["y"]
        return (
            lax.rem(y, 2) * 32 + pos["x"] * 8 + pos["z"],
            lax.div(y, 2) * 2 + core,
        )

    def member(self, by):
        spot = lax.rem(self.me + by, GROUP)
        return self.device({**self.pos, "y": lax.rem(spot, 4)}, lax.div(spot, 4))

    def step(self, axis, by):
        return self.steps[(axis, by % SIZE[axis])]

    def beside(self, axis, by):
        return self.devices[(axis, by)]


def place(where):
    return tuple(where[axis] for axis in AXES)


def gather(buffer, here, sets, send_sems, recv_sems, sent, keep=None):
    mine = buffer.at[here.core]
    other = buffer.at[1 - here.core]

    def copy(index, source, into, target):
        return pltpu.make_async_remote_copy(
            src_ref=source,
            dst_ref=into,
            send_sem=send_sems.at[index],
            recv_sem=recv_sems.at[index],
            device_id=target,
            device_id_type=MESH,
        )

    def start(index, source, into, target):
        made = copy(index, source, into, target)
        made.start()
        sent.append(made)

    def set_block(q, m, f):
        part, row, rows = sets[q]
        middle, final = PARTS[part]
        where = {
            middle: here.step(middle, -m),
            final: here.step(final, -f),
            "z": pl.ds(row, rows),
        }
        return mine.at[place(where)]

    def launch(q):
        middle, final = PARTS[sets[q][0]]
        own = set_block(q, 0, 0)
        for m in NEAR:
            start(7 + q * 15 + m - 1, own, own, here.beside(middle, m))
        for f in NEAR:
            start(10 + q * 15 + f - 1, own, own, here.beside(final, f))

    def arrive(*offsets):
        for offset in offsets:
            came = mine.at[place({**here.pos, "z": OFFSETS.index(offset)})]
            copy(7 - offset, came, came, here.sibling).wait_recv()

    def forward(q):
        final = PARTS[sets[q][0]][1]
        for m in (1, 3, 2):
            came = set_block(q, m, 0)
            copy(7 + q * 15 + m - 1, came, came, here.sibling).wait_recv()
            for f in NEAR:
                start(13 + q * 15 + (m - 1) * 3 + f - 1, came, came, here.beside(final, f))

    def finish(q):
        for m in (0, 1, 3, 2):
            for f in (1, 3, 2):
                index = (10 if m == 0 else 13 + (m - 1) * 3) + q * 15 + f - 1
                came = set_block(q, m, f)
                copy(index, came, came, here.sibling).wait_recv()

    def hand_on(number):
        row = PAIRS[number][1]
        ref = mine.at[:, :, row : row + 2]
        start(97 + number, ref, ref, here.sibling)

    own = mine.at[place({**here.pos, "z": 0})]
    for by in (1, 7, 2, 6, 3, 5, 4):
        into = mine.at[place({**here.pos, "z": OFFSETS.index(8 - by)})]
        start(by - 1, own, into, here.beside("z", by))
    if len(sets) == 6:
        launch(0)
        yield
        arrive(1)
        launch(1)
        arrive(7)
        launch(2)
        arrive(6)
        launch(3)
        forward(0)
        arrive(2, 3)
        launch(4)
        arrive(5, 4)
        launch(5)
        for q in (1, 2, 3, 4, 5):
            forward(q)
        completing = (1, 3, 4, 5)
    else:
        yield
        arrive(1)
        launch(0)
        arrive(7, 6)
        launch(1)
        arrive(2, 3)
        launch(2)
        arrive(5, 4)
        launch(3)
        for q in range(4):
            forward(q)
        completing = (0, 1, 2, 3)
    for q in range(len(sets)):
        finish(q)
        if q in completing:
            hand_on(completing.index(q))
            if keep is not None:
                keep(completing.index(q), here.core)
    for number, (_, row, rows) in enumerate(PAIRS):
        came = other.at[:, :, row : row + rows]
        copy(97 + number, came, came, here.sibling).wait_recv()
        if keep is not None:
            keep(number, 1 - here.core)


class Scatter:
    def __init__(self, sums, boxes, here, send_sems, recv_sems, sent):
        self.sums, self.boxes, self.here = sums, boxes, here
        self.send_sems, self.recv_sems, self.sent = send_sems, recv_sems, sent

    def copy(self, index, source, into, target):
        return pltpu.make_async_remote_copy(
            src_ref=source,
            dst_ref=into,
            send_sem=self.send_sems.at[index],
            recv_sem=self.recv_sems.at[index],
            device_id=target,
            device_id_type=MESH,
        )

    def start(self, *what):
        made = self.copy(*what)
        made.start()
        self.sent.append(made)

    def rows(self, q):
        return pl.ds(PAIRS[q][1], PAIRS[q][2])

    def piece(self, q, by_first, by_second):
        second, first = PARTS[PAIRS[q][0]]
        where = {
            first: self.here.step(first, by_first),
            second: self.here.step(second, by_second),
            "z": self.rows(q),
        }
        return place(where)

    def first_x(self, q, by, by_second):
        self.start(
            q * 15 + (by - 1) * 4 + by_second,
            self.sums.at[self.piece(q, by, by_second)],
            self.boxes[0].at[by - 1, by_second, self.rows(q)],
            self.here.beside("x", by),
        )

    def first_y(self, q, by):
        self.start(
            q * 15 + by - 1,
            self.sums.at[self.here.step("y", by), :, self.rows(q)],
            self.boxes[0].at[by - 1, :, self.rows(q)],
            self.here.beside("y", by),
        )

    def came(self, index, into):
        self.copy(index, into, into, self.here.sibling).wait_recv()

    def second(self, q, by_second, fresh):
        where = self.piece(q, 0, by_second)
        total = self.sums[where].astype(F32)
        rows = self.rows(q)
        for by in (1, 3, 2):
            if PAIRS[q][0] == 0:
                into = (by - 1, by_second, rows)
                self.came(q * 15 + (by - 1) * 4 + by_second, self.boxes[0].at[into])
            else:
                into = (by - 1, self.here.step("x", by_second), rows)
                if fresh:
                    self.came(q * 15 + by - 1, self.boxes[0].at[by - 1, :, rows])
            total = total + self.boxes[0][into].astype(F32)
        if by_second:
            self.sums[where] = total.astype(BF16)
            self.start(
                q * 15 + 12 + by_second - 1,
                self.sums.at[where],
                self.boxes[1].at[by_second - 1, rows],
                self.here.beside(PARTS[PAIRS[q][0]][0], by_second),
            )
            return
        for by in (1, 3, 2):
            into = (by - 1, rows)
            self.came(q * 15 + 12 + by - 1, self.boxes[1].at[into])
            total = total + self.boxes[1][into].astype(F32)
        self.sums[where] = total.astype(BF16)

    def third(self, *offsets):
        for by in offsets:
            self.start(
                60 + by - 1,
                self.sums.at[place({**self.here.pos, "z": OFFSETS.index(by)})],
                self.boxes[2].at[by - 1],
                self.here.beside("z", by),
            )

    def total(self):
        total = self.sums[place({**self.here.pos, "z": 0})].astype(F32)
        for by in (4, 3, 5, 2, 6, 1, 7):
            self.came(60 + by - 1, self.boxes[2].at[by - 1])
            total = total + self.boxes[2][by - 1].astype(F32)
        return total


def kernel(
    tokens,
    target,
    master_up,
    master_down,
    tangent_up,
    tangent_down,
    tokens_out,
    residuals_out,
    both_t,
    grads_t,
    v_master_up,
    v_master_down,
    v_tangent_up,
    v_tangent_down,
    group,
    folded,
    all_tokens,
    weights_up,
    weights_down,
    acc,
    both,
    slopes_ref,
    bend_ref,
    outgoing,
    incoming,
    sums,
    residuals,
    *rest,
):
    boxes = rest[:3]
    in_sems, out_sems, pair_send, pair_recv, group_send, group_recv = rest[3:9]
    first_send, first_recv, scatter_send, scatter_recv, second_send, second_recv = rest[9:]

    here = Here()
    core, pos, me = here.core, here.pos, here.me
    sent = []

    loads = []
    pairs = (
        (master_up, v_master_up),
        (tangent_up, v_tangent_up),
        (master_down, v_master_down),
        (tangent_down, v_tangent_down),
    )
    for number, (source, into) in enumerate(pairs):
        made = pltpu.make_async_copy(source, into, in_sems.at[number])
        made.start()
        loads.append(made)

    barrier = pltpu.get_barrier_semaphore()
    peers = [here.member(by) for by in range(1, GROUP)]
    peers += [here.beside("x", by) for by in range(1, 4)]
    peers += [here.beside("z", by) for by in range(1, 8)]
    for peer in peers:
        pl.semaphore_signal(barrier, inc=1, device_id=peer, device_id_type=MESH)

    def fold(rows):
        rows = rows.astype(F32)
        pieces = [rows[:, k * WIDE : (k + 1) * WIDE] for k in range(GROUP)]
        return jnp.concatenate(pieces, axis=0).astype(BF16)

    folded[core, pos["y"], pos["x"], 0] = fold(tokens[...])
    group[me] = fold(target[...])

    loads[0].wait()
    loads[1].wait()
    zeros_up = jnp.zeros((PAD - HID, 768), BF16)
    for k in range(4):
        columns = slice(k * 768, (k + 1) * 768)
        weights_up[k, 0:HID] = v_master_up[:, columns].astype(BF16)
        weights_up[k, HID:PAD] = zeros_up
        weights_up[k, PAD : PAD + HID] = v_tangent_up[:, columns]
        weights_up[k, PAD + HID :] = zeros_up
    pl.semaphore_wait(barrier, len(peers))

    first = gather(folded, here, PAIRS, first_send, first_recv, sent)
    next(first)

    def group_copy(by, spot):
        return pltpu.make_async_remote_copy(
            src_ref=group.at[spot],
            dst_ref=group.at[spot],
            send_sem=group_send.at[by],
            recv_sem=group_recv.at[by],
            device_id=here.member(by),
            device_id_type=MESH,
        )

    for by in range(1, GROUP):
        made = group_copy(by, me)
        made.start()
        sent.append(made)

    loads[2].wait()
    loads[3].wait()
    zeros_low = jnp.zeros((PAD - HID, 2 * WIDE), BF16)
    zeros_half = jnp.zeros((HID, WIDE), BF16)
    for spot in range(GROUP):
        columns = slice(spot * WIDE, (spot + 1) * WIDE)
        weight = v_master_down[:, columns].astype(BF16)
        weights_down[spot, 0:HID, 0:WIDE] = weight
        weights_down[spot, 0:HID, WIDE:] = v_tangent_down[:, columns]
        weights_down[spot, HID:PAD] = zeros_low
        weights_down[spot, PAD : PAD + HID, 0:WIDE] = zeros_half
        weights_down[spot, PAD : PAD + HID, WIDE:] = weight
        weights_down[spot, PAD + HID :] = zeros_low

    for _ in first:
        pass

    row = lax.broadcasted_iota(jnp.int32, (128, 128), 0)
    column = lax.broadcasted_iota(jnp.int32, (128, 128), 1)
    token = lax.rem(row, 16)
    pick = column == lax.div(token, 2) * 16 + lax.div(row, 16) * 2 + lax.rem(token, 2)
    pick = pick.astype(F32).astype(BF16)

    @pl.loop(0, 4)
    def _(x):
        for z in range(8):
            blocks = folded[:, :, x, z].reshape(128, WIDE)
            rows = jnp.dot(pick, blocks, preferred_element_type=F32).astype(BF16)
            all_tokens[:, x, z] = rows.reshape(GROUP, 16, WIDE)

    stores = [pltpu.make_async_copy(all_tokens, tokens_out, out_sems.at[0])]
    stores[0].start()

    acc[...] = jnp.zeros_like(acc)

    @pl.loop(0, 4)
    def _(k):
        blocks = [all_tokens[2 * k + lower].reshape(TOKENS, WIDE) for lower in range(2)]
        acc[...] += lax.dot_general(
            jnp.concatenate(blocks, axis=1),
            weights_up[k],
            (((1,), (1,)), ((), ())),
            preferred_element_type=F32,
        )

    @pl.loop(0, 4)
    def _(x):
        span = pl.ds(pl.multiple_of(x * 128, 128), 128)
        pre_tangent = acc[span, PAD:]
        activated, slopes, bending = gelu_parts(acc[span, :PAD])
        slopes_ref[span] = slopes
        bend_ref[span] = bending * pre_tangent
        pair = jnp.concatenate([activated, slopes * pre_tangent], axis=1)
        both[x] = pair.astype(BF16).reshape(8, 16, 2 * PAD)

    def pair_copy(far, by):
        return pltpu.make_async_remote_copy(
            src_ref=outgoing.at[far, by],
            dst_ref=incoming.at[far, by],
            send_sem=pair_send.at[far, by],
            recv_sem=pair_recv.at[far, by],
            device_id=here.sibling,
            device_id_type=MESH,
        )

    turns = (1, 3, 2, 0)
    shape = (4, 4, 16, 2 * WIDE)

    def product(far, spot):
        left = both[:, 4 * far : 4 * far + 4].reshape(TOKENS // 2, 2 * PAD)
        return jnp.dot(left, weights_down[spot], preferred_element_type=F32)

    for far in (1, 0):
        for by in turns:
            spot = (1 - core) * 4 + here.step("y", by)
            outgoing[far, by] = product(far, spot).astype(BF16).reshape(shape)
            made = pair_copy(far, by)
            made.start()
            sent.append(made)

    scatter = Scatter(sums, boxes, here, scatter_send, scatter_recv, sent)
    for far in (1, 0):
        for by in turns:
            pair_copy(far, by).wait_recv()
            y = here.step("y", by)
            block = product(far, core * 4 + y)
            block = block + incoming[far, by].astype(F32).reshape(TOKENS // 2, 2 * WIDE)
            sums[y, :, 4 * far : 4 * far + 4] = block.astype(BF16).reshape(shape)
            for to in NEAR:
                scatter.first_x(2 * far, to, by)
            if by:
                scatter.first_y(2 * far + 1, by)

    both_t[...] = both[...].reshape(TOKENS, 2 * PAD).astype(F32).T.astype(BF16)
    for by in turns:
        for q in (2, 3):
            scatter.second(q, by, by == turns[0])
    scatter.third(4, 3, 5, 2)
    for by in turns:
        for q in (1, 0):
            scatter.second(q, by, by == turns[0])
            if by == 0:
                scatter.third(*((6, 7) if q else (1,)))
    total = scatter.total()

    for by in range(1, GROUP):
        group_copy(by, lax.rem(me + GROUP - by, GROUP)).wait_recv()
    row = lax.broadcasted_iota(jnp.int32, (16, 128), 0)
    column = lax.broadcasted_iota(jnp.int32, (16, 128), 1)
    pick = (column == lax.div(row, 2) * 16 + me * 2 + lax.rem(row, 2)).astype(F32).astype(BF16)
    goal = jnp.dot(pick, group[...].reshape(128, WIDE), preferred_element_type=F32)
    pair = jnp.concatenate([total[:, WIDE:], total[:, :WIDE] - goal], axis=1)
    residuals[core, pos["y"], pos["x"], 0] = pair.astype(BF16)

    def keep(number, core):
        row = PAIRS[number][1]
        made = pltpu.make_async_copy(
            residuals.at[core, :, :, row : row + 2],
            residuals_out.at[core, :, :, row : row + 2],
            out_sems.at[len(stores)],
        )
        made.start()
        stores.append(made)

    earlier = list(sent)
    sent.clear()
    last = gather(residuals, here, SETS, second_send, second_recv, sent, keep)
    next(last)
    for made in earlier:
        made.wait_send()
    for _ in last:
        pass

    acc[...] = jnp.zeros_like(acc)

    @pl.loop(0, GROUP)
    def _(spot):
        acc[...] += lax.dot_general(
            residuals[lax.div(spot, 4), lax.rem(spot, 4)].reshape(TOKENS, 2 * WIDE),
            weights_down[spot],
            (((1,), (1,)), ((), ())),
            preferred_element_type=F32,
        )

    for k in range(4):
        span = slice(k * 128, (k + 1) * 128)
        back_dot, back_grad = acc[span, :PAD], acc[span, PAD:]
        slopes = slopes_ref[span]
        grad_pre = (back_grad * slopes).T.astype(BF16)
        grad_pre_dot = (back_dot * slopes + back_grad * bend_ref[span]).T.astype(BF16)
        grads_t[0:PAD, span] = grad_pre
        grads_t[PAD:, span] = grad_pre_dot

    for made in stores:
        made.wait()
    for made in sent:
        made.wait_send()


def update(
    grads_t,
    both_t,
    tokens,
    residuals,
    tangent_up,
    tangent_down,
    moment_up,
    moment_down,
    curve_up,
    curve_down,
    step_up,
    step_down,
    moment_up_next,
    moment_down_next,
    curve_up_next,
    curve_down_next,
):
    loss_scale = 1.0 / math.sqrt(TOKENS)
    wide = [tokens[k].reshape(TOKENS, WIDE) for k in range(2)]
    up = jnp.dot(grads_t[...], jnp.concatenate(wide, axis=1), preferred_element_type=F32)
    step_up[...], moment_up_next[...], curve_up_next[...] = refresh(
        moment_up[...],
        curve_up[...],
        loss_scale * up[:HID],
        loss_scale * up[PAD : PAD + HID],
        tangent_up[...],
    )
    grad, hvp = [], []
    for k in range(2):
        down = jnp.dot(
            both_t[...],
            residuals[k].reshape(TOKENS, 2 * WIDE),
            preferred_element_type=F32,
        )
        grad.append(down[:HID, WIDE:])
        hvp.append(down[:HID, :WIDE] + down[PAD : PAD + HID, WIDE:])
    step_down[...], moment_down_next[...], curve_down_next[...] = refresh(
        moment_down[...],
        curve_down[...],
        loss_scale * jnp.concatenate(grad, axis=1),
        loss_scale * jnp.concatenate(hvp, axis=1),
        tangent_down[...],
    )


def per_device(
    tokens,
    target,
    master_up,
    master_down,
    tangent_up,
    tangent_down,
    moment_up,
    moment_down,
    curve_up,
    curve_down,
):
    wide32 = jax.ShapeDtypeStruct((HID, D), F32)
    wide16 = jax.ShapeDtypeStruct((HID, D), BF16)
    blocks = (4, 4, 8, 16)
    any_spec = pl.BlockSpec(memory_space=pl.ANY)
    vmem_spec = pl.BlockSpec(memory_space=pltpu.VMEM)
    scratch = [pltpu.VMEM((HID, D), F32)] * 2 + [pltpu.VMEM((HID, D), BF16)] * 2
    scratch += [
        pltpu.VMEM((GROUP, 16, WIDE), BF16),
        pltpu.VMEM((2,) + blocks + (WIDE,), BF16),
        pltpu.VMEM((GROUP, 4, 8, 16, WIDE), BF16),
        pltpu.VMEM((4, 2 * PAD, 768), BF16),
        pltpu.VMEM((GROUP, 2 * PAD, 2 * WIDE), BF16),
        pltpu.VMEM((TOKENS, 2 * PAD), F32),
        pltpu.VMEM((4, 8, 16, 2 * PAD), BF16),
        pltpu.VMEM((TOKENS, PAD), F32),
        pltpu.VMEM((TOKENS, PAD), F32),
        pltpu.VMEM((2, 4, 4, 4, 16, 2 * WIDE), BF16),
        pltpu.VMEM((2, 4, 4, 4, 16, 2 * WIDE), BF16),
        pltpu.VMEM(blocks + (2 * WIDE,), BF16),
        pltpu.VMEM((2,) + blocks + (2 * WIDE,), BF16),
        pltpu.VMEM((3, 4, 8, 16, 2 * WIDE), BF16),
        pltpu.VMEM((3, 8, 16, 2 * WIDE), BF16),
        pltpu.VMEM((7, 16, 2 * WIDE), BF16),
    ]
    dma = pltpu.SemaphoreType.DMA
    scratch += [
        dma((4,)),
        dma((9,)),
        dma((2, 4)),
        dma((2, 4)),
        dma((GROUP,)),
        dma((GROUP,)),
        dma((GATHER_COUNT,)),
        dma((GATHER_COUNT,)),
        dma((SCATTER_COUNT,)),
        dma((SCATTER_COUNT,)),
        dma((GATHER_COUNT,)),
        dma((GATHER_COUNT,)),
    ]
    all_tokens, residuals, both_t, grads_t = pl.pallas_call(
        kernel,
        out_shape=(
            jax.ShapeDtypeStruct((GROUP, 4, 8, 16, WIDE), BF16),
            jax.ShapeDtypeStruct((2,) + blocks + (2 * WIDE,), BF16),
            jax.ShapeDtypeStruct((2 * PAD, TOKENS), BF16),
            jax.ShapeDtypeStruct((2 * PAD, TOKENS), BF16),
        ),
        in_specs=[vmem_spec] * 2 + [any_spec] * 4,
        out_specs=(any_spec, any_spec, vmem_spec, vmem_spec),
        scratch_shapes=scratch,
        compiler_params=pltpu.CompilerParams(
            collective_id=0, has_side_effects=True, vmem_limit_bytes=62 * 1024 * 1024
        ),
        cost_estimate=pl.CostEstimate(
            flops=3_000_000_000, bytes_accessed=16_000_000, transcendentals=131072
        ),
    )(tokens, target, master_up, master_down, tangent_up, tangent_down)
    residuals = residuals.reshape((GROUP, 4, 8, 16, 2 * WIDE))
    whole = pl.BlockSpec((2 * PAD, TOKENS), lambda spot: (0, 0))
    part = pl.BlockSpec((HID, 2 * WIDE), lambda spot: (0, spot))
    return pl.pallas_call(
        update,
        grid=(GROUP // 2,),
        out_shape=(wide32, wide32, wide16, wide16, wide16, wide16),
        in_specs=[
            whole,
            whole,
            pl.BlockSpec((2, 4, 8, 16, WIDE), lambda spot: (spot, 0, 0, 0, 0)),
            pl.BlockSpec((2, 4, 8, 16, 2 * WIDE), lambda spot: (spot, 0, 0, 0, 0)),
        ]
        + [part] * 6,
        out_specs=(part,) * 6,
        compiler_params=pltpu.CompilerParams(vmem_limit_bytes=62 * 1024 * 1024),
        cost_estimate=pl.CostEstimate(
            flops=1_500_000_000, bytes_accessed=18_000_000, transcendentals=0
        ),
    )(
        grads_t,
        both_t,
        all_tokens,
        residuals,
        tangent_up,
        tangent_down,
        moment_up,
        moment_down,
        curve_up,
        curve_down,
    )


def solution(mesh):
    rows = P(("dp", "tensor"), None)
    return jax.shard_map(
        per_device, mesh=mesh, in_specs=(rows,) * 10, out_specs=(rows,) * 6, check_vma=False
    )
```

time: 116 us -> 112 us (0.966)
  local copies, waits for them, and re-layouts: 7.65 us -> 0 us
  Pallas kernels: 107 us -> 111 us
    unnamed x16 -> x0, local copies, waits for them, and re-layouts: 7.65 us -> none
    pallas_call x1 -> x2, Pallas kernels: 107 us -> 111 us  [the longest x1 102 us: per_device(): pl.pallas_call(kernel, out_shape=(jax.ShapeDtypeStruct((GROUP, 4, 8, 16,...]
where the time goes in v3:
time: 112 us
  Pallas kernels  111 us (99%)
    pallas_call x1, Pallas kernels, per_device(): pl.pallas_call(kernel, out_shape=(jax.ShapeDtypeStruct((GROUP, 4, 8, 16,...  102 us
    pallas_call x1, Pallas kernels, per_device(): pl.pallas_call(update, grid=(GROUP // 2,), out_shape=(wide32, wide32, wid...  8.96 us

profile of v3, /device:TPU:1, one launch (start us, length us, event | category | flops | bytes accessed | tf_op | source)
XLA Modules:
  0.0 111.5 jit_solution(203808649077395804)
XLA Ops:
  0.6 101.9 %shard_map.145 = (bf16[8,4,8,16,384]{4,3,2,1,0:T(8,128)(2,1)}, bf16[2,4,4,8,16,768]{5,4,3,2,1,0:T(8,128)(2,1)}, bf16[256,512]{1,0:T(8,128)(2,1)}, bf16[256,512]{1,0:T(8,128)(2,1)}) custom-call(bf16[2,3072]{1,0:T(2,128)(2,1)} %tokens.1, bf16[2,3072]{1,0:T(2,128)(2,1)} %target.1, f32[96,3072]{1,0:T(8,128)} %master_up.1, f32[96,3072]{1,0:T(8,128)} %master_down.1, ...), custom_call_target="tpu_custom_call" | custom-call | flops 3000000000 | bytes 16000000 | tf_op jit(solution)/shard_map/pallas_call | solution.py:660
  102.6 9.0 %shard_map.146 = (f32[96,3072]{1,0:T(8,128)}, f32[96,3072]{1,0:T(8,128)}, bf16[96,3072]{1,0:T(8,128)(2,1)}, bf16[96,3072]{1,0:T(8,128)(2,1)}, bf16[96,3072]{1,0:T(8,128)(2,1)}, /*index=5*/bf16[96,3072]{1,0:T(8,128)(2,1)}) custom-call(bf16[256,512]{1,0:T(8,128)(2,1)} %get-tuple-element.10.grads_t, bf16[256,512]{1,0:T(8,128)(2,1)} %get-tuple-element.11.both_t, ...), custom_call_target="tpu_custom_call" | custom-call | flops 1500000000 | bytes 18000000 | tf_op jit(solution)/shard_map/pallas_call | solution.py:681

commit v4 on v3

--- a/solution.py
+++ b/solution.py
@@ -21,8 +21,10 @@
 OFFSETS = (0, 1, 7, 6, 2, 3, 5, 4)
 PAIRS = ((0, 0, 2), (1, 2, 2), (0, 4, 2), (1, 6, 2))
 SETS = ((0, 0, 1), (0, 1, 1), (1, 2, 1), (1, 3, 1), (0, 4, 2), (1, 6, 2))
-GATHER_COUNT = 7 + 6 * 15 + 4
-SCATTER_COUNT = 4 * 15 + 7
+MAIN = 640
+SIDE = pl.ds(MAIN, 2 * WIDE - MAIN)
+GATHER_COUNT = 7 + 6 * 15 + 4 + 1 + 3 + 3 + 7
+SCATTER_COUNT = 4 * 15 + 7 + 7 + 3 + 3
 
 beta_first = 0.965
 beta_second = 0.99
@@ -103,6 +105,8 @@
 
 
 def gather(buffer, here, sets, send_sems, recv_sems, sent, keep=None):
+    side = keep is not None
+    columns = pl.ds(0, MAIN if side else WIDE)
     mine = buffer.at[here.core]
     other = buffer.at[1 - here.core]
 
@@ -129,7 +133,7 @@
             final: here.step(final, -f),
             "z": pl.ds(row, rows),
         }
-        return mine.at[place(where)]
+        return mine.at[place(where) + (slice(None), columns)]
 
     def launch(q):
         middle, final = PARTS[sets[q][0]]
@@ -141,7 +145,8 @@
 
     def arrive(*offsets):
         for offset in offsets:
-            came = mine.at[place({**here.pos, "z": OFFSETS.index(offset)})]
+            where = place({**here.pos, "z": OFFSETS.index(offset)})
+            came = mine.at[where + (slice(None), columns)]
             copy(7 - offset, came, came, here.sibling).wait_recv()
 
     def forward(q):
@@ -161,23 +166,58 @@
 
     def hand_on(number):
         row = PAIRS[number][1]
-        ref = mine.at[:, :, row : row + 2]
+        ref = mine.at[:, :, row : row + 2, :, columns]
         start(97 + number, ref, ref, here.sibling)
 
-    own = mine.at[place({**here.pos, "z": 0})]
+    here_y, here_x = here.pos["y"], here.pos["x"]
+
+    def side_x():
+        ref = mine.at[here_y, here_x, 0, :, SIDE]
+        for by in NEAR:
+            start(102 + by - 1, ref, ref, here.beside("x", by))
+
+    def side_y():
+        for by in NEAR:
+            ref = mine.at[here_y, here.step("x", -by), 0, :, SIDE]
+            copy(102 + by - 1, ref, ref, here.sibling).wait_recv()
+        ref = mine.at[here_y, :, 0, :, SIDE]
+        for by in NEAR:
+            start(105 + by - 1, ref, ref, here.beside("y", by))
+
+    def side_z():
+        for by in NEAR:
+            ref = mine.at[here.step("y", -by), :, 0, :, SIDE]
+            copy(105 + by - 1, ref, ref, here.sibling).wait_recv()
+        for by in (4, 3, 5, 2, 6, 1, 7):
+            into = mine.at[:, :, OFFSETS.index(8 - by), :, SIDE]
+            start(108 + by - 1, mine.at[:, :, 0, :, SIDE], into, here.beside("z", by))
+
+    def side_end():
+        for by in (1, 7, 2, 6, 3, 5, 4):
+            ref = mine.at[:, :, OFFSETS.index(8 - by), :, SIDE]
+            copy(108 + by - 1, ref, ref, here.sibling).wait_recv()
+        ref = mine.at[:, :, :, :, SIDE]
+        start(101, ref, ref, here.sibling)
+        keep(None, here.core)
+
+    if side:
+        side_x()
+    own = mine.at[place({**here.pos, "z": 0}) + (slice(None), columns)]
     for by in (1, 7, 2, 6, 3, 5, 4):
-        into = mine.at[place({**here.pos, "z": OFFSETS.index(8 - by)})]
+        into = mine.at[place({**here.pos, "z": OFFSETS.index(8 - by)}) + (slice(None), columns)]
         start(by - 1, own, into, here.beside("z", by))
     if len(sets) == 6:
         launch(0)
         yield
         arrive(1)
         launch(1)
+        side_y()
         arrive(7)
         launch(2)
         arrive(6)
         launch(3)
         forward(0)
+        side_z()
         arrive(2, 3)
         launch(4)
         arrive(5, 4)
@@ -200,15 +240,21 @@
         completing = (0, 1, 2, 3)
     for q in range(len(sets)):
         finish(q)
+        if side and q == 3:
+            side_end()
         if q in completing:
             hand_on(completing.index(q))
             if keep is not None:
                 keep(completing.index(q), here.core)
     for number, (_, row, rows) in enumerate(PAIRS):
-        came = other.at[:, :, row : row + rows]
+        came = other.at[:, :, row : row + rows, :, columns]
         copy(97 + number, came, came, here.sibling).wait_recv()
         if keep is not None:
             keep(number, 1 - here.core)
+    if side:
+        came = other.at[:, :, :, :, SIDE]
+        copy(101, came, came, here.sibling).wait_recv()
+        keep(None, 1 - here.core)
 
 
 class Scatter:
@@ -241,7 +287,7 @@
             second: self.here.step(second, by_second),
             "z": self.rows(q),
         }
-        return place(where)
+        return place(where) + (slice(None), pl.ds(0, MAIN))
 
     def first_x(self, q, by, by_second):
         self.start(
@@ -254,7 +300,7 @@
     def first_y(self, q, by):
         self.start(
             q * 15 + by - 1,
-            self.sums.at[self.here.step("y", by), :, self.rows(q)],
+            self.sums.at[self.here.step("y", by), :, self.rows(q), :, pl.ds(0, MAIN)],
             self.boxes[0].at[by - 1, :, self.rows(q)],
             self.here.beside("y", by),
         )
@@ -294,13 +340,61 @@
         for by in offsets:
             self.start(
                 60 + by - 1,
-                self.sums.at[place({**self.here.pos, "z": OFFSETS.index(by)})],
+                self.sums.at[self.own(OFFSETS.index(by))],
                 self.boxes[2].at[by - 1],
                 self.here.beside("z", by),
             )
 
+    def own(self, row):
+        return place({**self.here.pos, "z": row}) + (slice(None), pl.ds(0, MAIN))
+
+    def side_z(self, *offsets):
+        for by in offsets:
+            self.start(
+                67 + by - 1,
+                self.sums.at[:, :, OFFSETS.index(by), :, SIDE],
+                self.boxes[3].at[by - 1],
+                self.here.beside("z", by),
+            )
+
+    def side_y(self):
+        total = self.sums[:, :, 0, :, SIDE].astype(F32)
+        for by in (1, 7, 2, 6, 3, 5, 4):
+            self.came(67 + by - 1, self.boxes[3].at[by - 1])
+            total = total + self.boxes[3][by - 1].astype(F32)
+        self.sums[:, :, 0, :, SIDE] = total.astype(BF16)
+        for by in NEAR:
+            self.start(
+                74 + by - 1,
+                self.sums.at[self.here.step("y", by), :, 0, :, SIDE],
+                self.boxes[4].at[by - 1],
+                self.here.beside("y", by),
+            )
+
+    def side_x(self):
+        y = self.here.pos["y"]
+        total = self.sums[y, :, 0, :, SIDE].astype(F32)
+        for by in (1, 3, 2):
+            self.came(74 + by - 1, self.boxes[4].at[by - 1])
+            total = total + self.boxes[4][by - 1].astype(F32)
+        self.sums[y, :, 0, :, SIDE] = total.astype(BF16)
+        for by in NEAR:
+            self.start(
+                77 + by - 1,
+                self.sums.at[y, self.here.step("x", by), 0, :, SIDE],
+                self.boxes[5].at[by - 1],
+                self.here.beside("x", by),
+            )
+
+    def side_total(self):
+        total = self.sums[self.here.pos["y"], self.here.pos["x"], 0, :, SIDE].astype(F32)
+        for by in (1, 3, 2):
+            self.came(77 + by - 1, self.boxes[5].at[by - 1])
+            total = total + self.boxes[5][by - 1].astype(F32)
+        return total
+
     def total(self):
-        total = self.sums[place({**self.here.pos, "z": 0})].astype(F32)
+        total = self.sums[self.own(0)].astype(F32)
         for by in (4, 3, 5, 2, 6, 1, 7):
             self.came(60 + by - 1, self.boxes[2].at[by - 1])
             total = total + self.boxes[2][by - 1].astype(F32)
@@ -337,9 +431,9 @@
     residuals,
     *rest,
 ):
-    boxes = rest[:3]
-    in_sems, out_sems, pair_send, pair_recv, group_send, group_recv = rest[3:9]
-    first_send, first_recv, scatter_send, scatter_recv, second_send, second_recv = rest[9:]
+    boxes = rest[:6]
+    in_sems, out_sems, pair_send, pair_recv, group_send, group_recv = rest[6:12]
+    first_send, first_recv, scatter_send, scatter_recv, second_send, second_recv = rest[12:]
 
     here = Here()
     core, pos, me = here.core, here.pos, here.me
@@ -493,6 +587,7 @@
                 scatter.first_x(2 * far, to, by)
             if by:
                 scatter.first_y(2 * far + 1, by)
+        scatter.side_z(*((4, 3, 5, 2) if far else (6, 1, 7)))
 
     both_t[...] = both[...].reshape(TOKENS, 2 * PAD).astype(F32).T.astype(BF16)
     for by in turns:
@@ -504,7 +599,11 @@
             scatter.second(q, by, by == turns[0])
             if by == 0:
                 scatter.third(*((6, 7) if q else (1,)))
+        if by == 3:
+            scatter.side_y()
+    scatter.side_x()
     total = scatter.total()
+    total = jnp.concatenate([total, scatter.side_total()], axis=1)
 
     for by in range(1, GROUP):
         group_copy(by, lax.rem(me + GROUP - by, GROUP)).wait_recv()
@@ -516,10 +615,12 @@
     residuals[core, pos["y"], pos["x"], 0] = pair.astype(BF16)
 
     def keep(number, core):
-        row = PAIRS[number][1]
+        row, rows, columns = 0, 8, SIDE
+        if number is not None:
+            row, rows, columns = PAIRS[number][1], 2, pl.ds(0, MAIN)
         made = pltpu.make_async_copy(
-            residuals.at[core, :, :, row : row + 2],
-            residuals_out.at[core, :, :, row : row + 2],
+            residuals.at[core, :, :, row : row + rows, :, columns],
+            residuals_out.at[core, :, :, row : row + rows, :, columns],
             out_sems.at[len(stores)],
         )
         made.start()
@@ -638,14 +739,17 @@
         pltpu.VMEM((2, 4, 4, 4, 16, 2 * WIDE), BF16),
         pltpu.VMEM(blocks + (2 * WIDE,), BF16),
         pltpu.VMEM((2,) + blocks + (2 * WIDE,), BF16),
-        pltpu.VMEM((3, 4, 8, 16, 2 * WIDE), BF16),
-        pltpu.VMEM((3, 8, 16, 2 * WIDE), BF16),
-        pltpu.VMEM((7, 16, 2 * WIDE), BF16),
+        pltpu.VMEM((3, 4, 8, 16, MAIN), BF16),
+        pltpu.VMEM((3, 8, 16, MAIN), BF16),
+        pltpu.VMEM((7, 16, MAIN), BF16),
+        pltpu.VMEM((7, 4, 4, 16, 2 * WIDE - MAIN), BF16),
+        pltpu.VMEM((3, 4, 16, 2 * WIDE - MAIN), BF16),
+        pltpu.VMEM((3, 16, 2 * WIDE - MAIN), BF16),
     ]
     dma = pltpu.SemaphoreType.DMA
     scratch += [
         dma((4,)),
-        dma((9,)),
+        dma((11,)),
         dma((2, 4)),
         dma((2, 4)),
         dma((GROUP,)),

time: 112 us -> 106 us (0.946)
  Pallas kernels: 111 us -> 106 us
    pallas_call x1, Pallas kernels: 102 us -> 96.6 us  [per_device(): pl.pallas_call(kernel, out_shape=(jax.ShapeDtypeStruct((GROUP, 4, 8, 16,...]
where the time goes in v4:
time: 106 us
  Pallas kernels  106 us (100%)
    pallas_call x1, Pallas kernels, per_device(): pl.pallas_call(kernel, out_shape=(jax.ShapeDtypeStruct((GROUP, 4, 8, 16,...  96.6 us
    pallas_call x1, Pallas kernels, per_device(): pl.pallas_call(update, grid=(GROUP // 2,), out_shape=(wide32, wide32, wid...  8.96 us

profile of v4, /device:TPU:1, one launch (start us, length us, event | category | flops | bytes accessed | tf_op | source)
XLA Modules:
  0.0 106.2 jit_solution(13587782362556706718)
XLA Ops:
  0.6 96.6 %shard_map.145 = (bf16[8,4,8,16,384]{4,3,2,1,0:T(8,128)(2,1)}, bf16[2,4,4,8,16,768]{5,4,3,2,1,0:T(8,128)(2,1)}, bf16[256,512]{1,0:T(8,128)(2,1)}, bf16[256,512]{1,0:T(8,128)(2,1)}) custom-call(bf16[2,3072]{1,0:T(2,128)(2,1)} %tokens.1, bf16[2,3072]{1,0:T(2,128)(2,1)} %target.1, f32[96,3072]{1,0:T(8,128)} %master_up.1, f32[96,3072]{1,0:T(8,128)} %master_down.1, ...), custom_call_target="tpu_custom_call" | custom-call | flops 3000000000 | bytes 16000000 | tf_op jit(solution)/shard_map/pallas_call | solution.py:764
  97.3 9.0 %shard_map.146 = (f32[96,3072]{1,0:T(8,128)}, f32[96,3072]{1,0:T(8,128)}, bf16[96,3072]{1,0:T(8,128)(2,1)}, bf16[96,3072]{1,0:T(8,128)(2,1)}, bf16[96,3072]{1,0:T(8,128)(2,1)}, /*index=5*/bf16[96,3072]{1,0:T(8,128)(2,1)}) custom-call(bf16[256,512]{1,0:T(8,128)(2,1)} %get-tuple-element.10.grads_t, bf16[256,512]{1,0:T(8,128)(2,1)} %get-tuple-element.11.both_t, ...), custom_call_target="tpu_custom_call" | custom-call | flops 1500000000 | bytes 18000000 | tf_op jit(solution)/shard_map/pallas_call | solution.py:785

commit v5 on v4

--- a/solution.py
+++ b/solution.py
@@ -679,8 +679,9 @@
     curve_up_next,
     curve_down_next,
 ):
+    first = 2 * pl.program_id(0)
     loss_scale = 1.0 / math.sqrt(TOKENS)
-    wide = [tokens[k].reshape(TOKENS, WIDE) for k in range(2)]
+    wide = [tokens[first + k].reshape(TOKENS, WIDE) for k in range(2)]
     up = jnp.dot(grads_t[...], jnp.concatenate(wide, axis=1), preferred_element_type=F32)
     step_up[...], moment_up_next[...], curve_up_next[...] = refresh(
         moment_up[...],
@@ -693,7 +694,7 @@
     for k in range(2):
         down = jnp.dot(
             both_t[...],
-            residuals[k].reshape(TOKENS, 2 * WIDE),
+            residuals[first + k].reshape(TOKENS, 2 * WIDE),
             preferred_element_type=F32,
         )
         grad.append(down[:HID, WIDE:])
@@ -764,16 +765,16 @@
     all_tokens, residuals, both_t, grads_t = pl.pallas_call(
         kernel,
         out_shape=(
-            jax.ShapeDtypeStruct((GROUP, 4, 8, 16, WIDE), BF16),
-            jax.ShapeDtypeStruct((2,) + blocks + (2 * WIDE,), BF16),
-            jax.ShapeDtypeStruct((2 * PAD, TOKENS), BF16),
-            jax.ShapeDtypeStruct((2 * PAD, TOKENS), BF16),
+            pltpu.VMEM((GROUP, 4, 8, 16, WIDE), BF16),
+            pltpu.VMEM((2,) + blocks + (2 * WIDE,), BF16),
+            pltpu.VMEM((2 * PAD, TOKENS), BF16),
+            pltpu.VMEM((2 * PAD, TOKENS), BF16),
         ),
         in_specs=[vmem_spec] * 2 + [any_spec] * 4,
-        out_specs=(any_spec, any_spec, vmem_spec, vmem_spec),
+        out_specs=(vmem_spec,) * 4,
         scratch_shapes=scratch,
         compiler_params=pltpu.CompilerParams(
-            collective_id=0, has_side_effects=True, vmem_limit_bytes=62 * 1024 * 1024
+            collective_id=0, has_side_effects=True, vmem_limit_bytes=49 * 1024 * 1024
         ),
         cost_estimate=pl.CostEstimate(
             flops=3_000_000_000, bytes_accessed=16_000_000, transcendentals=131072
@@ -789,12 +790,12 @@
         in_specs=[
             whole,
             whole,
-            pl.BlockSpec((2, 4, 8, 16, WIDE), lambda spot: (spot, 0, 0, 0, 0)),
-            pl.BlockSpec((2, 4, 8, 16, 2 * WIDE), lambda spot: (spot, 0, 0, 0, 0)),
+            vmem_spec,
+            vmem_spec,
         ]
         + [part] * 6,
         out_specs=(part,) * 6,
-        compiler_params=pltpu.CompilerParams(vmem_limit_bytes=62 * 1024 * 1024),
+        compiler_params=pltpu.CompilerParams(vmem_limit_bytes=30 * 1024 * 1024),
         cost_estimate=pl.CostEstimate(
             flops=1_500_000_000, bytes_accessed=18_000_000, transcendentals=0
         ),

time: 106 us -> 102 us (0.962)
  Pallas kernels: 106 us -> 101 us
    pallas_call x1, Pallas kernels: 8.96 us -> 4.77 us  [per_device(): pl.pallas_call(update, grid=(GROUP // 2,), out_shape=(wide32, wide32, wid...]
where the time goes in v5:
time: 102 us
  Pallas kernels  101 us (99%)
    pallas_call x1, Pallas kernels, per_device(): pl.pallas_call(kernel, out_shape=(pltpu.VMEM((GROUP, 4, 8, 16, WIDE), BF1...  96.5 us
    pallas_call x1, Pallas kernels, per_device(): pl.pallas_call(update, grid=(GROUP // 2,), out_shape=(wide32, wide32, wid...  4.77 us

profile of v5, /device:TPU:1, one launch (start us, length us, event | category | flops | bytes accessed | tf_op | source)
XLA Modules:
  0.0 102.0 jit_solution(11704097644306396397)
XLA Ops:
  0.6 0.0 copy-start.1
  0.6 0.0 copy-start
  0.7 0.0 copy-start.5
  0.7 0.0 copy-start.4
  0.7 0.0 copy-start.3
  0.7 0.0 copy-start.2
  0.7 96.5 %shard_map.145 = (bf16[8,4,8,16,384]{4,3,2,1,0:T(8,128)(2,1)S(1)}, bf16[2,4,4,8,16,768]{5,4,3,2,1,0:T(8,128)(2,1)S(1)}, bf16[256,512]{1,0:T(8,128)(2,1)S(1)}, bf16[256,512]{1,0:T(8,128)(2,1)S(1)}) custom-call(bf16[2,3072]{1,0:T(2,128)(2,1)} %tokens.1, bf16[2,3072]{1,0:T(2,128)(2,1)} %target.1, f32[96,3072]{1,0:T(8,128)} %master_up.1, ...), custom_call_target="tpu_custom_call" | custom-call | flops 3000000000 | bytes 16000000 | tf_op jit(solution)/shard_map/pallas_call | solution.py:765
  97.2 0.0 copy-done.1
  97.2 0.0 copy-done
  97.2 0.0 copy-done.5
  97.2 0.0 copy-done.4
  97.2 0.0 copy-done.3
  97.2 0.0 copy-done.2
  97.2 4.8 %shard_map.146 = (f32[96,3072]{1,0:T(8,128)}, f32[96,3072]{1,0:T(8,128)}, bf16[96,3072]{1,0:T(8,128)(2,1)}, bf16[96,3072]{1,0:T(8,128)(2,1)}, bf16[96,3072]{1,0:T(8,128)(2,1)}, /*index=5*/bf16[96,3072]{1,0:T(8,128)(2,1)}) custom-call(bf16[256,512]{1,0:T(8,128)(2,1)S(1)} %get-tuple-element.10.grads_t, bf16[256,512]{1,0:T(8,128)(2,1)S(1)} %get-tuple-element.11.both_t, ...), custom_call_target="tpu_custom_call" | custom-call | flops 1500000000 | bytes 18000000 | tf_op jit(solution)/shard_map/pallas_call | solution.py:786
Async XLA Ops:
  0.6 96.5 %copy-start.1 = (bf16[96,3072]{1,0:T(8,128)(2,1)S(1)}, bf16[96,3072]{1,0:T(8,128)(2,1)}, u32[]{:S(2)}) copy-start(bf16[96,3072]{1,0:T(8,128)(2,1)} %tangent_down.3) | copy-start | bytes 1769476
  0.6 96.5 %copy-start = (bf16[96,3072]{1,0:T(8,128)(2,1)S(1)}, bf16[96,3072]{1,0:T(8,128)(2,1)}, u32[]{:S(2)}) copy-start(bf16[96,3072]{1,0:T(8,128)(2,1)} %tangent_up.3) | copy-start | bytes 1769476
  0.7 96.5 %copy-start.5 = (bf16[96,3072]{1,0:T(8,128)(2,1)S(1)}, bf16[96,3072]{1,0:T(8,128)(2,1)}, u32[]{:S(2)}) copy-start(bf16[96,3072]{1,0:T(8,128)(2,1)} %curve_down.1) | copy-start | bytes 1769476
  0.7 96.5 %copy-start.4 = (bf16[96,3072]{1,0:T(8,128)(2,1)S(1)}, bf16[96,3072]{1,0:T(8,128)(2,1)}, u32[]{:S(2)}) copy-start(bf16[96,3072]{1,0:T(8,128)(2,1)} %curve_up.1) | copy-start | bytes 1769476
  0.7 96.5 %copy-start.3 = (bf16[96,3072]{1,0:T(8,128)(2,1)S(1)}, bf16[96,3072]{1,0:T(8,128)(2,1)}, u32[]{:S(2)}) copy-start(bf16[96,3072]{1,0:T(8,128)(2,1)} %moment_down.1) | copy-start | bytes 1769476
  0.7 96.5 %copy-start.2 = (bf16[96,3072]{1,0:T(8,128)(2,1)S(1)}, bf16[96,3072]{1,0:T(8,128)(2,1)}, u32[]{:S(2)}) copy-start(bf16[96,3072]{1,0:T(8,128)(2,1)} %moment_up.1) | copy-start | bytes 1769476

commit v6 on v5

--- a/solution.py
+++ b/solution.py
@@ -412,6 +412,8 @@
     residuals_out,
     both_t,
     grads_t,
+    v_tokens,
+    v_target,
     v_master_up,
     v_master_down,
     v_tangent_up,
@@ -439,8 +441,17 @@
     core, pos, me = here.core, here.pos, here.me
     sent = []
 
+    barrier = pltpu.get_barrier_semaphore()
+    peers = [here.member(by) for by in range(1, GROUP)]
+    peers += [here.beside("x", by) for by in range(1, 4)]
+    peers += [here.beside("z", by) for by in range(1, 8)]
+    for peer in peers:
+        pl.semaphore_signal(barrier, inc=1, device_id=peer, device_id_type=MESH)
+
     loads = []
     pairs = (
+        (tokens, v_tokens),
+        (target, v_target),
         (master_up, v_master_up),
         (tangent_up, v_tangent_up),
         (master_down, v_master_down),
@@ -451,23 +462,18 @@
         made.start()
         loads.append(made)
 
-    barrier = pltpu.get_barrier_semaphore()
-    peers = [here.member(by) for by in range(1, GROUP)]
-    peers += [here.beside("x", by) for by in range(1, 4)]
-    peers += [here.beside("z", by) for by in range(1, 8)]
-    for peer in peers:
-        pl.semaphore_signal(barrier, inc=1, device_id=peer, device_id_type=MESH)
-
     def fold(rows):
         rows = rows.astype(F32)
         pieces = [rows[:, k * WIDE : (k + 1) * WIDE] for k in range(GROUP)]
         return jnp.concatenate(pieces, axis=0).astype(BF16)
 
-    folded[core, pos["y"], pos["x"], 0] = fold(tokens[...])
-    group[me] = fold(target[...])
-
     loads[0].wait()
     loads[1].wait()
+    folded[core, pos["y"], pos["x"], 0] = fold(v_tokens[...])
+    group[me] = fold(v_target[...])
+
+    loads[2].wait()
+    loads[3].wait()
     zeros_up = jnp.zeros((PAD - HID, 768), BF16)
     for k in range(4):
         columns = slice(k * 768, (k + 1) * 768)
@@ -495,8 +501,8 @@
         made.start()
         sent.append(made)
 
-    loads[2].wait()
-    loads[3].wait()
+    loads[4].wait()
+    loads[5].wait()
     zeros_low = jnp.zeros((PAD - HID, 2 * WIDE), BF16)
     zeros_half = jnp.zeros((HID, WIDE), BF16)
     for spot in range(GROUP):
@@ -567,6 +573,7 @@
         left = both[:, 4 * far : 4 * far + 4].reshape(TOKENS // 2, 2 * PAD)
         return jnp.dot(left, weights_down[spot], preferred_element_type=F32)
 
+    scatter = Scatter(sums, boxes, here, scatter_send, scatter_recv, sent)
     for far in (1, 0):
         for by in turns:
             spot = (1 - core) * 4 + here.step("y", by)
@@ -574,9 +581,6 @@
             made = pair_copy(far, by)
             made.start()
             sent.append(made)
-
-    scatter = Scatter(sums, boxes, here, scatter_send, scatter_recv, sent)
-    for far in (1, 0):
         for by in turns:
             pair_copy(far, by).wait_recv()
             y = here.step("y", by)
@@ -725,7 +729,8 @@
     blocks = (4, 4, 8, 16)
     any_spec = pl.BlockSpec(memory_space=pl.ANY)
     vmem_spec = pl.BlockSpec(memory_space=pltpu.VMEM)
-    scratch = [pltpu.VMEM((HID, D), F32)] * 2 + [pltpu.VMEM((HID, D), BF16)] * 2
+    scratch = [pltpu.VMEM((2, D), BF16)] * 2
+    scratch += [pltpu.VMEM((HID, D), F32)] * 2 + [pltpu.VMEM((HID, D), BF16)] * 2
     scratch += [
         pltpu.VMEM((GROUP, 16, WIDE), BF16),
         pltpu.VMEM((2,) + blocks + (WIDE,), BF16),
@@ -749,7 +754,7 @@
     ]
     dma = pltpu.SemaphoreType.DMA
     scratch += [
-        dma((4,)),
+        dma((6,)),
         dma((11,)),
         dma((2, 4)),
         dma((2, 4)),
@@ -770,7 +775,7 @@
             pltpu.VMEM((2 * PAD, TOKENS), BF16),
             pltpu.VMEM((2 * PAD, TOKENS), BF16),
         ),
-        in_specs=[vmem_spec] * 2 + [any_spec] * 4,
+        in_specs=[any_spec] * 6,
         out_specs=(vmem_spec,) * 4,
         scratch_shapes=scratch,
         compiler_params=pltpu.CompilerParams(

time: 102 us -> 98.9 us (0.970)
  Pallas kernels: 101 us -> 98.1 us
    pallas_call x1, Pallas kernels: 96.5 us -> 93.3 us  [per_device(): pl.pallas_call(kernel, out_shape=(pltpu.VMEM((GROUP, 4, 8, 16, WIDE), BF1...]
where the time goes in v6:
time: 98.9 us
  Pallas kernels  98.1 us (99%)
    pallas_call x1, Pallas kernels, per_device(): pl.pallas_call(kernel, out_shape=(pltpu.VMEM((GROUP, 4, 8, 16, WIDE), BF1...  93.3 us
    pallas_call x1, Pallas kernels, per_device(): pl.pallas_call(update, grid=(GROUP // 2,), out_shape=(wide32, wide32, wid...  4.77 us

profile of v6, /device:TPU:1, one launch (start us, length us, event | category | flops | bytes accessed | tf_op | source)
XLA Modules:
  0.0 98.9 jit_solution(18214349675416910145)
XLA Ops:
  0.6 0.0 copy-start.1
  0.6 0.0 copy-start
  0.7 0.0 copy-start.5
  0.7 0.0 copy-start.4
  0.7 0.0 copy-start.3
  0.7 0.0 copy-start.2
  0.7 93.3 %shard_map.145 = (bf16[8,4,8,16,384]{4,3,2,1,0:T(8,128)(2,1)S(1)}, bf16[2,4,4,8,16,768]{5,4,3,2,1,0:T(8,128)(2,1)S(1)}, bf16[256,512]{1,0:T(8,128)(2,1)S(1)}, bf16[256,512]{1,0:T(8,128)(2,1)S(1)}) custom-call(bf16[2,3072]{1,0:T(2,128)(2,1)} %tokens.1, bf16[2,3072]{1,0:T(2,128)(2,1)} %target.1, f32[96,3072]{1,0:T(8,128)} %master_up.1, ...), custom_call_target="tpu_custom_call" | custom-call | flops 3000000000 | bytes 16000000 | tf_op jit(solution)/shard_map/pallas_call | solution.py:770
  94.0 0.0 copy-done.1
  94.0 0.0 copy-done
  94.0 0.0 copy-done.5
  94.1 0.0 copy-done.4
  94.1 0.0 copy-done.3
  94.1 0.0 copy-done.2
  94.1 4.8 %shard_map.146 = (f32[96,3072]{1,0:T(8,128)}, f32[96,3072]{1,0:T(8,128)}, bf16[96,3072]{1,0:T(8,128)(2,1)}, bf16[96,3072]{1,0:T(8,128)(2,1)}, bf16[96,3072]{1,0:T(8,128)(2,1)}, /*index=5*/bf16[96,3072]{1,0:T(8,128)(2,1)}) custom-call(bf16[256,512]{1,0:T(8,128)(2,1)S(1)} %get-tuple-element.10.grads_t, bf16[256,512]{1,0:T(8,128)(2,1)S(1)} %get-tuple-element.11.both_t, ...), custom_call_target="tpu_custom_call" | custom-call | flops 1500000000 | bytes 18000000 | tf_op jit(solution)/shard_map/pallas_call | solution.py:791
Async XLA Ops:
  0.6 93.4 %copy-start.1 = (bf16[96,3072]{1,0:T(8,128)(2,1)S(1)}, bf16[96,3072]{1,0:T(8,128)(2,1)}, u32[]{:S(2)}) copy-start(bf16[96,3072]{1,0:T(8,128)(2,1)} %tangent_down.3) | copy-start | bytes 1769476
  0.6 93.4 %copy-start = (bf16[96,3072]{1,0:T(8,128)(2,1)S(1)}, bf16[96,3072]{1,0:T(8,128)(2,1)}, u32[]{:S(2)}) copy-start(bf16[96,3072]{1,0:T(8,128)(2,1)} %tangent_up.3) | copy-start | bytes 1769476
  0.7 93.4 %copy-start.5 = (bf16[96,3072]{1,0:T(8,128)(2,1)S(1)}, bf16[96,3072]{1,0:T(8,128)(2,1)}, u32[]{:S(2)}) copy-start(bf16[96,3072]{1,0:T(8,128)(2,1)} %curve_down.1) | copy-start | bytes 1769476
  0.7 93.4 %copy-start.4 = (bf16[96,3072]{1,0:T(8,128)(2,1)S(1)}, bf16[96,3072]{1,0:T(8,128)(2,1)}, u32[]{:S(2)}) copy-start(bf16[96,3072]{1,0:T(8,128)(2,1)} %curve_up.1) | copy-start | bytes 1769476
  0.7 93.4 %copy-start.3 = (bf16[96,3072]{1,0:T(8,128)(2,1)S(1)}, bf16[96,3072]{1,0:T(8,128)(2,1)}, u32[]{:S(2)}) copy-start(bf16[96,3072]{1,0:T(8,128)(2,1)} %moment_down.1) | copy-start | bytes 1769476
  0.7 93.4 %copy-start.2 = (bf16[96,3072]{1,0:T(8,128)(2,1)S(1)}, bf16[96,3072]{1,0:T(8,128)(2,1)}, u32[]{:S(2)}) copy-start(bf16[96,3072]{1,0:T(8,128)(2,1)} %moment_up.1) | copy-start | bytes 1769476

commit v7 on v6

--- a/solution.py
+++ b/solution.py
@@ -593,6 +593,12 @@
                 scatter.first_y(2 * far + 1, by)
         scatter.side_z(*((4, 3, 5, 2) if far else (6, 1, 7)))
 
+    for by in range(1, GROUP):
+        group_copy(by, lax.rem(me + GROUP - by, GROUP)).wait_recv()
+    row = lax.broadcasted_iota(jnp.int32, (16, 128), 0)
+    column = lax.broadcasted_iota(jnp.int32, (16, 128), 1)
+    pick = (column == lax.div(row, 2) * 16 + me * 2 + lax.rem(row, 2)).astype(F32).astype(BF16)
+    goal = jnp.dot(pick, group[...].reshape(128, WIDE), preferred_element_type=F32)
     both_t[...] = both[...].reshape(TOKENS, 2 * PAD).astype(F32).T.astype(BF16)
     for by in turns:
         for q in (2, 3):
@@ -609,12 +615,6 @@
     total = scatter.total()
     total = jnp.concatenate([total, scatter.side_total()], axis=1)
 
-    for by in range(1, GROUP):
-        group_copy(by, lax.rem(me + GROUP - by, GROUP)).wait_recv()
-    row = lax.broadcasted_iota(jnp.int32, (16, 128), 0)
-    column = lax.broadcasted_iota(jnp.int32, (16, 128), 1)
-    pick = (column == lax.div(row, 2) * 16 + me * 2 + lax.rem(row, 2)).astype(F32).astype(BF16)
-    goal = jnp.dot(pick, group[...].reshape(128, WIDE), preferred_element_type=F32)
     pair = jnp.concatenate([total[:, WIDE:], total[:, :WIDE] - goal], axis=1)
     residuals[core, pos["y"], pos["x"], 0] = pair.astype(BF16)
 

time: 98.9 us -> 98.8 us (level)
  no operation moved by 1% of the time
where the time goes in v7:
time: 98.8 us; the launch traced here: 98.7 us
  Pallas kernels  97.9 us (99%)
    pallas_call x1, Pallas kernels, per_device(): pl.pallas_call(kernel, out_shape=(pltpu.VMEM((GROUP, 4, 8, 16, WIDE), BF1...  93.2 us
    pallas_call x1, Pallas kernels, per_device(): pl.pallas_call(update, grid=(GROUP // 2,), out_shape=(wide32, wide32, wid...  4.77 us

profile of v7, /device:TPU:1, one launch (start us, length us, event | category | flops | bytes accessed | tf_op | source)
XLA Modules:
  0.0 98.7 jit_solution(4122441074357404799)
XLA Ops:
  0.6 0.0 copy-start.1
  0.6 0.0 copy-start
  0.7 0.0 copy-start.5
  0.7 0.0 copy-start.4
  0.7 0.0 copy-start.3
  0.7 0.0 copy-start.2
  0.7 93.2 %shard_map.145 = (bf16[8,4,8,16,384]{4,3,2,1,0:T(8,128)(2,1)S(1)}, bf16[2,4,4,8,16,768]{5,4,3,2,1,0:T(8,128)(2,1)S(1)}, bf16[256,512]{1,0:T(8,128)(2,1)S(1)}, bf16[256,512]{1,0:T(8,128)(2,1)S(1)}) custom-call(bf16[2,3072]{1,0:T(2,128)(2,1)} %tokens.1, bf16[2,3072]{1,0:T(2,128)(2,1)} %target.1, f32[96,3072]{1,0:T(8,128)} %master_up.1, ...), custom_call_target="tpu_custom_call" | custom-call | flops 3000000000 | bytes 16000000 | tf_op jit(solution)/shard_map/pallas_call | solution.py:770
  93.9 0.0 copy-done.1
  93.9 0.0 copy-done
  93.9 0.0 copy-done.5
  93.9 0.0 copy-done.4
  93.9 0.0 copy-done.3
  93.9 0.0 copy-done.2
  93.9 4.8 %shard_map.146 = (f32[96,3072]{1,0:T(8,128)}, f32[96,3072]{1,0:T(8,128)}, bf16[96,3072]{1,0:T(8,128)(2,1)}, bf16[96,3072]{1,0:T(8,128)(2,1)}, bf16[96,3072]{1,0:T(8,128)(2,1)}, /*index=5*/bf16[96,3072]{1,0:T(8,128)(2,1)}) custom-call(bf16[256,512]{1,0:T(8,128)(2,1)S(1)} %get-tuple-element.10.grads_t, bf16[256,512]{1,0:T(8,128)(2,1)S(1)} %get-tuple-element.11.both_t, ...), custom_call_target="tpu_custom_call" | custom-call | flops 1500000000 | bytes 18000000 | tf_op jit(solution)/shard_map/pallas_call | solution.py:791
Async XLA Ops:
  0.6 93.2 %copy-start.1 = (bf16[96,3072]{1,0:T(8,128)(2,1)S(1)}, bf16[96,3072]{1,0:T(8,128)(2,1)}, u32[]{:S(2)}) copy-start(bf16[96,3072]{1,0:T(8,128)(2,1)} %tangent_down.3) | copy-start | bytes 1769476
  0.6 93.2 %copy-start = (bf16[96,3072]{1,0:T(8,128)(2,1)S(1)}, bf16[96,3072]{1,0:T(8,128)(2,1)}, u32[]{:S(2)}) copy-start(bf16[96,3072]{1,0:T(8,128)(2,1)} %tangent_up.3) | copy-start | bytes 1769476
  0.7 93.2 %copy-start.5 = (bf16[96,3072]{1,0:T(8,128)(2,1)S(1)}, bf16[96,3072]{1,0:T(8,128)(2,1)}, u32[]{:S(2)}) copy-start(bf16[96,3072]{1,0:T(8,128)(2,1)} %curve_down.1) | copy-start | bytes 1769476
  0.7 93.2 %copy-start.4 = (bf16[96,3072]{1,0:T(8,128)(2,1)S(1)}, bf16[96,3072]{1,0:T(8,128)(2,1)}, u32[]{:S(2)}) copy-start(bf16[96,3072]{1,0:T(8,128)(2,1)} %curve_up.1) | copy-start | bytes 1769476
  0.7 93.2 %copy-start.3 = (bf16[96,3072]{1,0:T(8,128)(2,1)S(1)}, bf16[96,3072]{1,0:T(8,128)(2,1)}, u32[]{:S(2)}) copy-start(bf16[96,3072]{1,0:T(8,128)(2,1)} %moment_down.1) | copy-start | bytes 1769476
  0.7 93.2 %copy-start.2 = (bf16[96,3072]{1,0:T(8,128)(2,1)S(1)}, bf16[96,3072]{1,0:T(8,128)(2,1)}, u32[]{:S(2)}) copy-start(bf16[96,3072]{1,0:T(8,128)(2,1)} %moment_up.1) | copy-start | bytes 1769476
